TPU v7x, 128 devices: a whole 4x4x4 slice. The times are simulated.
128 devices in a mesh: row: 8 (over x, core), col: 16 (over y, z).
Axes of the slice: x: 4, y: 4, z: 4, core: 2. Of those that a mesh axis runs over, the one named last changes fastest.
Arguments:
- eigvec_slab: bfloat16 [512, 131072], P('col', 'row'), may hold values from -1 to 1
- occupations: int32 [512], replicated, may hold values from 1 to 2
- energies: float32 [512], replicated, may hold values from -1.6 to -0.1
- tile_owner: int32 [2048], P(('row', 'col')), may hold values from -1 to 15, as said below
- margin_change: bfloat16 [4096, 3, 64, 128], P(('row', 'col')), may hold values from -0.23925781 to 0.23925781
- hamiltonian_change: bfloat16 [4096, 3, 64, 128], P(('row', 'col')), may hold values from -0.23925781 to 0.23925781
- basis_atom: int32 [131072], replicated, may hold values from 0 to 20479, as said below
Outputs:
- forces: float32 [3, 20480], P(None, ('row', 'col'))
Inputs may be any that keep to these rules, and one draw needn't show every extreme that they name: `tile_owner`: owners lie in the sending device's row; at most 2 row blocks of one device share an owner, and some device gives 2 to one owner. -1 marks a block outside the sparsity pattern. `basis_atom`: the basis functions of device d (functions d * 64 * 16 onward) belong to atoms d * 160 to (d + 1) * 160 - 1; ids never fall, every atom has 1 to 12 basis functions, and on every device one atom has exactly 12.
All inputs are finite; a program needn't handle non-finite values.
Results may differ from a plain program's by a relative error of at most 0.0035.
Values may be sent and summed in bfloat16 or wider, within the bound.
No kernel may reach another device: no remote copies, remote signals or barrier semaphores. Data moves between devices by JAX's collectives and lax.ppermute only.
A program may use at most 64 MiB of HBM per device.

v0:
```python
import jax
import jax.numpy as jnp
from jax import lax
from jax.sharding import PartitionSpec as P

ATOMS_DEV = 160


def spread(block, axis, source):
    block = jnp.where(lax.axis_index(axis) == source, block, jnp.zeros_like(block))
    return lax.psum(block, axis)


def per_device(
    eigvec_slab, occupations, energies, tile_owner, margin_change, hamiltonian_change, basis_atom
):
    columns = lax.axis_size("col")
    col_index = lax.axis_index("col")
    row_index = lax.axis_index("row")
    states_local = eigvec_slab.shape[0]
    blocks_here = tile_owner.shape[0]
    block_rows = margin_change.shape[2]
    panel_width = margin_change.shape[3]
    capacity = margin_change.shape[0] // columns
    occ = occupations.astype(jnp.float32)
    eweight = occ * energies
    occ_local = lax.dynamic_slice_in_dim(occ, col_index * states_local, states_local)
    ew_local = lax.dynamic_slice_in_dim(eweight, col_index * states_local, states_local)
    panel_local = spread(eigvec_slab[:, :panel_width], "row", 0)
    panel_float = panel_local.astype(jnp.float32)
    weights_local = jnp.concatenate(
        [
            (panel_float * occ_local[:, None]).astype(jnp.bfloat16),
            (panel_float * ew_local[:, None]).astype(jnp.bfloat16),
        ],
        axis=1,
    )
    density = lax.psum_scatter(
        lax.dot_general(
            eigvec_slab, weights_local, (((0,), (0,)), ((), ())), preferred_element_type=jnp.float32
        ),
        "col",
        scatter_dimension=0,
        tiled=True,
    ).astype(jnp.bfloat16)
    dtiles = density.reshape(blocks_here, block_rows, 2 * panel_width)
    same = tile_owner[:, None] == tile_owner[None, :]
    position = jnp.arange(blocks_here, dtype=jnp.int32)
    lower = position[None, :] < position[:, None]
    rank = jnp.sum((same & lower).astype(jnp.int32), axis=1)
    target_col = jnp.arange(columns, dtype=jnp.int32)
    target_slot = jnp.arange(capacity, dtype=jnp.int32)
    chosen = (tile_owner[None, None, :] == target_col[:, None, None]) & (
        rank[None, None, :] == target_slot[None, :, None]
    )
    chosen_int = chosen.astype(jnp.int32)
    present = jnp.sum(chosen_int, axis=2)
    local_block = jnp.where(present > 0, jnp.sum(chosen_int * position[None, None, :], axis=2), -1)
    outgoing = jnp.einsum(
        "dkj,jtq->dktq", chosen.astype(jnp.bfloat16), dtiles, preferred_element_type=jnp.float32
    ).astype(jnp.bfloat16)
    incoming, block_ids = (
        lax.all_to_all(outgoing, "col", split_axis=0, concat_axis=0, tiled=True),
        lax.all_to_all(local_block, "col", split_axis=0, concat_axis=0, tiled=True),
    )
    ochange = margin_change.reshape(columns, capacity, 3, block_rows, panel_width)
    hchange = hamiltonian_change.reshape(columns, capacity, 3, block_rows, panel_width)
    pdens = incoming[..., :panel_width]
    wdens = incoming[..., panel_width:]
    frow = jnp.einsum(
        "cktp,ckxtp->ckxt", pdens, hchange, preferred_element_type=jnp.float32
    ) - jnp.einsum("cktp,ckxtp->ckxt", wdens, ochange, preferred_element_type=jnp.float32)
    alive = (block_ids >= 0).astype(jnp.float32)
    frow = frow * alive[:, :, None, None]
    source_dev = row_index * columns + jnp.arange(columns, dtype=jnp.int32)
    first_row = (source_dev[:, None] * blocks_here + jnp.maximum(block_ids, 0)) * block_rows
    basis_rows = first_row[:, :, None] + jnp.arange(block_rows, dtype=jnp.int32)[None, None, :]
    atom_index = jnp.take(basis_atom, basis_rows.reshape(-1), axis=0)
    row_atoms = ATOMS_DEV * columns
    local_atom = atom_index - row_index * row_atoms
    frow_flat = jnp.transpose(frow, (0, 1, 3, 2)).reshape(-1, 3)
    partial_value = jax.ops.segment_sum(frow_flat, local_atom, num_segments=row_atoms).T
    summed = lax.psum_scatter(partial_value, "col", scatter_dimension=1, tiled=True)
    return 2.0 * summed


def solution(mesh):
    return jax.shard_map(
        per_device,
        mesh=mesh,
        in_specs=(
            P("col", "row"),
            P(),
            P(),
            P(("row", "col")),
            P(("row", "col"), None, None, None),
            P(("row", "col"), None, None, None),
            P(),
        ),
        out_specs=P(None, ("row", "col")),
        check_vma=False,
    )
```

profile of v0, /device:TPU:0, one launch (start us, length us, event | category | flops | bytes accessed | tf_op | source)
XLA Modules:
  0.0 269.4 jit_solution(9810649652966144637)
XLA Ops:
  6.5 0.8 convert_element_type.38
  7.3 0.7 convert_multiply_fusion.2
  8.2 0.7 slice_select_fusion
  8.9 14.9 %psum.7 = bf16[32,128]{1,0:T(8,128)(2,1)S(1)} all-reduce(bf16[32,128]{1,0:T(8,128)(2,1)S(1)} %slice_select_fusion), channel_id=1, replica_groups=mesh['row'=8,'col'=16] {'row'}, use_global_device_ids=true, to_apply=%region_3.4 | all-reduce | flops 4096 | bytes 16384 | tf_op jit(solution)/shard_map/psum | solution.py:11
  23.9 9.3 %convolution_bitcast_fusion = f32[16384,256]{0,1:T(8,128)} fusion(bf16[32,16384]{1,0:T(8,128)(2,1)} %param.7, bf16[32,128]{1,0:T(8,128)(2,1)S(1)} %get-tuple-element.10, bf16[32,128]{1,0:T(8,128)(2,1)S(1)} %get-tuple-element.9), kind=kOutput, calls=%fused_computation.2 | convolution fusion | flops 268468224 | bytes 17842176 | tf_op jit(solution)/shard_map/dot_general | solution.py:39
  33.3 0.6 copy-done.2
  34.2 0.7 copy.34
  34.9 8.0 %all-to-all-start = ((s32[16,1,2]{2,1,0:T(1,128)}), s32[16,1,2]{2,1,0:T(1,128)S(1)}, u32[]{:S(2)}, u32[]{:S(2)}) async-start(s32[16,1,2]{2,1,0:T(1,128)} %copy.34), calls=%async_computation | async-start | bytes 16384 | tf_op jit(solution)/shard_map/all_to_all | solution.py:64
  43.0 7.6 %all-to-all-done = s32[16,1,2]{2,1,0:T(1,128)S(1)} async-done(((s32[16,1,2]{2,1,0:T(1,128)}), s32[16,1,2]{2,1,0:T(1,128)S(1)}, u32[]{:S(2)}, u32[]{:S(2)}) %all-to-all-start) | async-done | bytes 160 | tf_op jit(solution)/shard_map/all_to_all | solution.py:64
  51.0 93.1 %reduce-scatter.5.cloned.1.call-done = f32[1024,256]{0,1:T(8,128)} async-done(((f32[16384,256]{0,1:T(8,128)}), f32[1024,256]{0,1:T(8,128)}) %reduce-scatter.5.cloned.1.call-update) | async-done | bytes 1048592 | tf_op jit(solution)/shard_map/reduce_scatter | solution.py:38
  144.1 1.3 convert_element_type.41
  145.4 0.2 copy.37
  145.6 0.4 convolution_convert_fusion
  146.0 1.3 copy.39
  147.4 5.2 %all-to-all-start.1 = ((bf16[16,2,64,256]{3,2,1,0:T(8,128)(2,1)}), bf16[16,2,64,256]{3,2,1,0:T(8,128)(2,1)S(1)}, u32[]{:S(2)}, u32[]{:S(2)}) async-start(bf16[16,2,64,256]{3,2,1,0:T(8,128)(2,1)} %copy.39), calls=%async_computation.2 | async-start | bytes 2097152 | tf_op jit(solution)/shard_map/all_to_all | solution.py:63
  152.7 11.8 %gather_fusion = s32[2048]{0:T(1024)S(1)} fusion(s32[131072]{0:T(1024)S(1)} %copy-done.1, s32[2048]{0:T(1024)S(1)} %broadcast_clamp_fusion), kind=kCustom, calls=%fused_computation | custom fusion | bytes 24576 | tf_op jit(solution)/shard_map/jit(_take)/gather | solution.py:78
  164.5 5.9 %all-to-all-done.1 = bf16[16,2,64,256]{3,2,1,0:T(8,128)(2,1)S(1)} async-done(((bf16[16,2,64,256]{3,2,1,0:T(8,128)(2,1)}), bf16[16,2,64,256]{3,2,1,0:T(8,128)(2,1)S(1)}, u32[]{:S(2)}, u32[]{:S(2)}) %all-to-all-start.1) | async-done | bytes 1048608 | tf_op jit(solution)/shard_map/all_to_all | solution.py:63
  170.4 0.3 slice_bitcast_fusion
  170.7 2.3 fusion.2
  173.0 2.3 fusion
  175.5 14.2 %scatter_custom_fusion = f32[2560,3]{1,0:T(8,128)} fusion(s32[2048]{0:T(1024)S(1)} %bitcast.46, f32[2048,3]{1,0:T(8,128)S(1)} %bitcast.41, f32[]{:T(128)} %constant.16.clone.1), kind=kCustom, calls=%fused_computation.11 | custom fusion | flops 6144 | bytes 30724 | tf_op jit(solution)/shard_map/scatter-add | solution.py:82
  189.8 71.2 %reduce-scatter.7.cloned.1.call-done = f32[160,3]{1,0:T(8,128)} async-done(((f32[2560,3]{1,0:T(8,128)}), f32[160,3]{1,0:T(8,128)}) %reduce-scatter.7.cloned.1.call-update) | async-done | bytes 1936
  261.0 1.0 copy.51
  261.9 0.6 broadcast_multiply_fusion
  (31 shorter events, 1.3 us)
Async XLA Ops:
  6.5 164.2 %copy-start = (bf16[32,3,64,128]{3,2,1,0:T(8,128)(2,1)S(1)}, bf16[32,3,64,128]{3,2,1,0:T(8,128)(2,1)}, u32[]{:S(2)}) copy-start(bf16[32,3,64,128]{3,2,1,0:T(8,128)(2,1)} %param.12) | copy-start | bytes 4718596
  6.5 137.5 %reduce-scatter.5.cloned.1.call-start = ((), (), s32[]{:S(2)}) async-start(), calls=%async_computation.4 | async-start | bytes 17825792 | tf_op jit(solution)/shard_map/reduce_scatter | solution.py:38
  33.2 0.7 copy-start.2
  34.9 15.6 %all-to-all-start = ((s32[16,1,2]{2,1,0:T(1,128)}), s32[16,1,2]{2,1,0:T(1,128)S(1)}, u32[]{:S(2)}, u32[]{:S(2)}) async-start(s32[16,1,2]{2,1,0:T(1,128)} %copy.34), calls=%async_computation | async-start | bytes 16384 | tf_op jit(solution)/shard_map/all_to_all | solution.py:64
  147.4 5.3 %copy-start.1 = (s32[131072]{0:T(1024)S(1)}, s32[131072]{0:T(1024)}, u32[]{:S(2)}) copy-start(s32[131072]{0:T(1024)} %param.13) | copy-start | bytes 1572868
  147.4 23.0 %all-to-all-start.1 = ((bf16[16,2,64,256]{3,2,1,0:T(8,128)(2,1)}), bf16[16,2,64,256]{3,2,1,0:T(8,128)(2,1)S(1)}, u32[]{:S(2)}, u32[]{:S(2)}) async-start(bf16[16,2,64,256]{3,2,1,0:T(8,128)(2,1)} %copy.39), calls=%async_computation.2 | async-start | bytes 2097152 | tf_op jit(solution)/shard_map/all_to_all | solution.py:63
  152.6 108.4 %reduce-scatter.7.cloned.1.call-start = ((), (), s32[]{:S(2)}) async-start(), calls=%async_computation.5 | async-start | bytes 1392640
  170.7 2.3 copy-start.3
Sparse Core Ops, SparseCore 0:
  33.4 110.6 reduce-scatter.4
  189.9 71.0 reduce-scatter.6
where the time goes:
time: 270 us; the launch traced here: 269 us
  waiting for transfers between devices  178 us (66%)
  other arithmetic  19.1 us (7%)
  local copies, waits for them, and re-layouts  16.4 us (6%)
  blocking collectives  14.9 us (6%)
  matrix products  14.4 us (5%)
  between operations  13.6 us (5%)
  starting transfers between devices  13.3 us (5%)
    reduce_scatter x1, waiting for transfers between devices, per_device(): lax.psum_scatter(lax.dot_general(eigvec_slab, weights_local, (((0,), (0,)...  93.1 us
    unnamed x3, waiting for transfers between devices  71.2 us
    psum x1, blocking collectives, spread(): return lax.psum(block, axis)  14.9 us
    scatter-add x1, other arithmetic, per_device(): jax.ops.segment_sum(frow_flat, local_atom, num_segments=row_atoms)  14.2 us
    gather x1, local copies, waits for them, and re-layouts, per_device(): atom_index = jnp.take(basis_atom, basis_rows.reshape(-1), axis=0)  11.8 us
    dot_general x1, matrix products, per_device(): lax.dot_general(eigvec_slab, weights_local, (((0,), (0,)), ((), ())), pre...  9.31 us
    all_to_all x1, starting transfers between devices, per_device(): lax.all_to_all(local_block, 'col', split_axis=0, concat_axis=0, tiled=True)  8.05 us
    all_to_all x1, waiting for transfers between devices, per_device(): lax.all_to_all(local_block, 'col', split_axis=0, concat_axis=0, tiled=True)  7.55 us
  transfers between devices with their start and end apart: 4, of which 4 were waited for; matrix products, arithmetic and copies ran while one was open for 5% of the time, Pallas kernels for 0%

commit v1 on v0

v1 whole, which is shorter than its diff:
```python
import jax
import jax.numpy as jnp
from jax import lax
from jax.experimental import pallas as pl
from jax.experimental.pallas import tpu as pltpu
from jax.sharding import PartitionSpec as P

ATOMS_DEV = 160
BF16 = jnp.bfloat16
F32 = jnp.float32
VMEM = pltpu.VMEM
SMEM = pltpu.SMEM


def whole(space=VMEM):
    return pl.BlockSpec(memory_space=space)


def slots_of(owner_ref, columns, blocks, shape):
    lane = lax.broadcasted_iota(jnp.int32, shape, 1)
    owner, rank = lane // 2, lane % 2
    first = jnp.full(shape, blocks, jnp.int32)
    last = jnp.full(shape, -1, jnp.int32)
    for b in range(blocks):
        last = jnp.where(owner == owner_ref[b], b, last)
        first = jnp.where(owner == owner_ref[blocks - 1 - b], blocks - 1 - b, first)
    second = jnp.where(last > first, last, blocks)
    return jnp.where(rank == 0, first, second)


def announce_kernel(owner_ref, panel_ref, out_ref):
    columns, _, width = out_ref.shape
    states = panel_ref.shape[0]
    out_ref[:, :states, :] = jnp.broadcast_to(panel_ref[...][None], (columns, states, width))
    table = slots_of(owner_ref, columns, owner_ref.shape[0], (16, width))
    out_ref[:, states:, :] = jnp.broadcast_to(table.astype(F32).astype(BF16)[None], (columns, 16, width))


def double_kernel(slab_ref, out_ref):
    columns, blocks, states, width = out_ref.shape
    blocks -= 1
    low = lax.broadcasted_iota(jnp.int32, (states, width), 1) < width // 2

    def home(c, carry):
        for j in range(blocks // 2):
            start = pl.multiple_of((c * (blocks // 2) + j) * width, width)
            tile = slab_ref[:, pl.ds(start, width)].astype(F32)
            turned = pltpu.roll(tile, width // 2, 1)
            out_ref[c, 2 * j] = jnp.where(low, tile, turned).astype(BF16)
            out_ref[c, 2 * j + 1] = jnp.where(low, turned, tile).astype(BF16)
        out_ref[c, blocks] = jnp.zeros((states, width), BF16)
        return carry

    lax.fori_loop(0, columns, home, 0)


def pack_kernel(table_ref, doubled_ref, out_ref):
    columns, homes, states, width = out_ref.shape
    low = lax.broadcasted_iota(jnp.int32, (states, width), 1) < width // 2

    def home(c, carry):
        for o in range(columns):
            left = doubled_ref[c, table_ref[c, 2 * o]]
            right = doubled_ref[c, table_ref[c, 2 * o + 1]]
            out_ref[o, c] = jnp.where(low, left, right)
        return carry

    lax.fori_loop(0, homes, home, 0)


def owner_kernel(slab_ref, weights_ref, ham_hbm, margin_hbm, out_ref, ham_ref, margin_ref, density_ref, sems):
    chunks, homes, states, width = slab_ref.shape
    half = width // 2
    copy_ham = pltpu.make_async_copy(ham_hbm, ham_ref, sems.at[0])
    copy_margin = pltpu.make_async_copy(margin_hbm, margin_ref, sems.at[1])
    copy_ham.start()
    copy_margin.start()
    for c in range(homes):
        pair = slab_ref[:, c].reshape(chunks * states, width)
        density_ref[c] = jnp.dot(weights_ref[...], pair, preferred_element_type=F32).astype(BF16)
    copy_ham.wait()
    copy_margin.wait()
    row = lax.broadcasted_iota(jnp.int32, (half, width), 0)
    lane = lax.broadcasted_iota(jnp.int32, (half, width), 1)
    masks = [lane == row + half * k for k in range(2)]
    for c in range(homes):
        change = jnp.concatenate(
            [ham_ref[2 * c : 2 * c + 2].reshape(6 * half, width), margin_ref[2 * c : 2 * c + 2].reshape(6 * half, width)],
            axis=1,
        )
        product = jnp.dot(change, density_ref[c], preferred_element_type=F32)
        product = product.reshape(2, 3, half, width)
        parts = []
        for x in range(3):
            kept = jnp.where(masks[0], product[0, x], 0.0) + jnp.where(masks[1], product[1, x], 0.0)
            parts.append(jnp.sum(kept, axis=0, keepdims=True))
        force = jnp.concatenate(parts + [jnp.zeros((5, width), F32)], axis=0)
        high = force.astype(BF16)
        low = (force - high.astype(F32)).astype(BF16)
        out_ref[c] = jnp.concatenate([high.astype(F32), low.astype(F32)], axis=0).astype(BF16)


def hot_kernel(owner_ref, atom_ref, out_ref, rows_ref):
    columns, width, atoms = out_ref.shape
    blocks = owner_ref.shape[0]
    half = width // 2
    lane = lax.broadcasted_iota(jnp.int32, (1, width), 1)
    rows_ref[...] = jnp.full(rows_ref.shape, -1, jnp.int32)
    for b in range(blocks):
        o = owner_ref[b]
        rank = jnp.int32(0)
        for earlier in range(b):
            rank = rank + (owner_ref[earlier] == o).astype(jnp.int32)

        @pl.when(o >= 0)
        def _():
            here = rows_ref[pl.ds(o, 1), :]
            rows_ref[pl.ds(o, 1), :] = jnp.where(lane // half == rank, atom_ref[b : b + 1, :], here)

    atom = lax.broadcasted_iota(jnp.int32, (atoms, width), 0)
    for o in range(columns):
        hot = (atom == rows_ref[o : o + 1, :]).astype(F32)
        out_ref[o] = hot.T.astype(BF16)


def gather_kernel(force_ref, hot_ref, out_ref):
    columns = force_ref.shape[0]
    total = jnp.zeros((force_ref.shape[1], hot_ref.shape[2]), F32)
    for o in range(columns):
        total = total + jnp.dot(force_ref[o], hot_ref[o], preferred_element_type=F32)
    out_ref[...] = 2.0 * (total[0:3, : out_ref.shape[1]] + total[8:11, : out_ref.shape[1]])


def per_device(
    eigvec_slab, occupations, energies, tile_owner, margin_change, hamiltonian_change, basis_atom
):
    columns = lax.axis_size("col")
    rows = lax.axis_size("row")
    col_index = lax.axis_index("col")
    row_index = lax.axis_index("row")
    states = eigvec_slab.shape[0]
    blocks = tile_owner.shape[0]
    block_rows = margin_change.shape[2]
    width = margin_change.shape[3]

    def swap(x):
        return lax.all_to_all(x, "col", split_axis=0, concat_axis=0, tiled=True)

    announced = pl.pallas_call(
        announce_kernel,
        grid=(1,),
        in_specs=[whole(SMEM), pl.BlockSpec((states, width), lambda i: (0, 0))],
        out_specs=pl.BlockSpec((columns, states + 16, width), lambda i: (0, 0, 0)),
        out_shape=jax.ShapeDtypeStruct((columns, states + 16, width), BF16),
    )(tile_owner, eigvec_slab)
    heard = swap(announced)
    doubled = pl.pallas_call(
        double_kernel,
        in_specs=[whole()],
        out_specs=whole(),
        out_shape=jax.ShapeDtypeStruct((columns, blocks + 1, states, width), BF16),
        cost_estimate=pl.CostEstimate(flops=4 << 20, bytes_accessed=3 << 20, transcendentals=0),
        compiler_params=pltpu.CompilerParams(vmem_limit_bytes=16 << 20),
    )(eigvec_slab)

    table = heard[:, states, : 2 * columns].astype(jnp.int32)
    packed = pl.pallas_call(
        pack_kernel,
        in_specs=[whole(SMEM), whole()],
        out_specs=whole(),
        out_shape=jax.ShapeDtypeStruct((columns, columns, states, width), BF16),
        compiler_params=pltpu.CompilerParams(vmem_limit_bytes=16 << 20),
    )(table, doubled)
    slabs = swap(packed)

    panel = heard[:, :states, :]
    panel = jnp.where(row_index == 0, panel, jnp.zeros_like(panel))
    reach = 1
    while reach < rows:
        panel = panel + lax.ppermute(panel, "row", [(i, i + reach) for i in range(reach)])
        reach *= 2
    occ = occupations.astype(F32)
    eweight = occ * energies
    panel_t = panel.reshape(columns * states, width).T.astype(F32)
    weights = jnp.concatenate(
        [(panel_t * occ[None, :]).astype(BF16), (panel_t * -eweight[None, :]).astype(BF16)], axis=0
    )

    device = row_index * columns + col_index
    atom = lax.dynamic_slice_in_dim(basis_atom, device * blocks * block_rows, blocks * block_rows)
    atom = (atom - device * ATOMS_DEV).reshape(blocks, block_rows)
    atom = jnp.concatenate([atom, atom], axis=1)
    atoms_padded = -(-ATOMS_DEV // 128) * 128
    hot = pl.pallas_call(
        hot_kernel,
        in_specs=[whole(SMEM), whole()],
        out_specs=whole(),
        out_shape=jax.ShapeDtypeStruct((columns, width, atoms_padded), BF16),
        scratch_shapes=[pltpu.VMEM((columns, width), jnp.int32)],
        cost_estimate=pl.CostEstimate(flops=4 << 20, bytes_accessed=1 << 20, transcendentals=0),
    )(tile_owner, atom)

    force = pl.pallas_call(
        owner_kernel,
        in_specs=[whole(), whole(), whole(pl.ANY), whole(pl.ANY)],
        out_specs=whole(),
        out_shape=jax.ShapeDtypeStruct((columns, 16, width), BF16),
        scratch_shapes=[
            pltpu.VMEM(hamiltonian_change.shape, BF16),
            pltpu.VMEM(margin_change.shape, BF16),
            pltpu.VMEM((columns, 2 * width, width), BF16),
            pltpu.SemaphoreType.DMA((2,)),
        ],
        compiler_params=pltpu.CompilerParams(vmem_limit_bytes=32 << 20),
    )(slabs, weights, hamiltonian_change, margin_change)

    returned = swap(force)
    return pl.pallas_call(
        gather_kernel,
        in_specs=[whole(), whole()],
        out_specs=whole(),
        out_shape=jax.ShapeDtypeStruct((3, ATOMS_DEV), F32),
    )(returned, hot)


def solution(mesh):
    return jax.shard_map(
        per_device,
        mesh=mesh,
        in_specs=(
            P("col", "row"),
            P(),
            P(),
            P(("row", "col")),
            P(("row", "col"), None, None, None),
            P(("row", "col"), None, None, None),
            P(),
        ),
        out_specs=P(None, ("row", "col")),
        check_vma=False,
    )
```

time: 270 us -> 74.1 us (0.27)
  waiting for transfers between devices: 178 us -> 34.4 us
  other arithmetic: 19.1 us -> 1.57 us
  blocking collectives: 14.9 us -> 0 us
  matrix products: 14.4 us -> 0 us
  between operations: 13.6 us -> 0.2 us
  Pallas kernels: 0 us -> 12.3 us
  local copies, waits for them, and re-layouts: 16.4 us -> 4.98 us
  starting transfers between devices: 13.3 us -> 20.1 us
    reduce_scatter x1 -> x0, waiting for transfers between devices: 93.1 us -> none  [per_device(): lax.psum_scatter(lax.dot_general(eigvec_slab, weights_local, (((0,), (0,)...]
    unnamed x3 -> x0, waiting for transfers between devices: 71.2 us -> none
    all_to_all x2 -> x3, waiting for transfers between devices: 13.4 us -> 28.8 us  [swap(): return lax.all_to_all(x, 'col', split_axis=0, concat_axis=0, tiled=True)]
    psum x1 -> x0, blocking collectives: 14.9 us -> none  [spread(): return lax.psum(block, axis)]
    dot_general x4 -> x0, matrix products: 14.4 us -> none  [the longest x1 9.31 us: per_device(): lax.dot_general(eigvec_slab, weights_local, (((0,), (0,)), ((), ())), pre...]
    scatter-add x1 -> x0, other arithmetic: 14.2 us -> none  [per_device(): jax.ops.segment_sum(frow_flat, local_atom, num_segments=row_atoms)]
    pallas_call x0 -> x6, Pallas kernels: none -> 12.3 us  [the longest x1 3.09 us: per_device(): pl.pallas_call(owner_kernel, in_specs=[whole(), whole(), whole(pl.ANY), w...]
    gather x1 -> x0, local copies, waits for them, and re-layouts: 11.8 us -> none  [per_device(): atom_index = jnp.take(basis_atom, basis_rows.reshape(-1), axis=0)]
  transfers between devices with their start and end apart: 4 -> 6, of which waited for: 4 -> 6; matrix products, arithmetic and copies ran while one was open for 5% -> 2% of each run, Pallas kernels for 0% -> 5%
where the time goes in v1:
time: 74.1 us; the launch traced here: 73.6 us
  waiting for transfers between devices  34.4 us (46%)
  starting transfers between devices  20.1 us (27%)
  Pallas kernels  12.3 us (17%)
  local copies, waits for them, and re-layouts  4.98 us (7%)
  other arithmetic  1.57 us (2%)
    all_to_all x3, waiting for transfers between devices, swap(): return lax.all_to_all(x, 'col', split_axis=0, concat_axis=0, tiled=True)  28.8 us
    all_to_all x3, starting transfers between devices, swap(): return lax.all_to_all(x, 'col', split_axis=0, concat_axis=0, tiled=True)  15.7 us
    ppermute x3, waiting for transfers between devices, per_device(): lax.ppermute(panel, 'row', [(i, i + reach) for i in range(reach)])  5.64 us
    unnamed x14, local copies, waits for them, and re-layouts  4.77 us
    ppermute x3, starting transfers between devices, per_device(): lax.ppermute(panel, 'row', [(i, i + reach) for i in range(reach)])  4.42 us
    pallas_call x1, Pallas kernels, per_device(): pl.pallas_call(owner_kernel, in_specs=[whole(), whole(), whole(pl.ANY), w...  3.09 us
    pallas_call x1, Pallas kernels, per_device(): pl.pallas_call(hot_kernel, in_specs=[whole(SMEM), whole()], out_specs=who...  2.3 us
    pallas_call x1, Pallas kernels, per_device(): pl.pallas_call(gather_kernel, in_specs=[whole(), whole()], out_specs=whol...  2.11 us
  transfers between devices with their start and end apart: 6, of which 6 were waited for; matrix products, arithmetic and copies ran while one was open for 2% of the time, Pallas kernels for 5%

profile of v1, /device:TPU:0, one launch (start us, length us, event | category | flops | bytes accessed | tf_op | source)
XLA Modules:
  0.0 73.6 jit_solution(13556057002402156168)
XLA Ops:
  0.0 1.5 %shard_map.73 = bf16[16,48,128]{2,1,0:T(8,128)(2,1)} custom-call(s32[16]{0:T(128)} %owner_ref.3, bf16[32,16384]{1,0:T(8,128)(2,1)} %slab_ref.1), custom_call_target="tpu_custom_call" | custom-call | tf_op jit(solution)/shard_map/pallas_call | solution.py:149
  1.5 8.1 %all-to-all-start = ((bf16[16,48,128]{2,1,0:T(8,128)(2,1)}), bf16[16,48,128]{2,1,0:T(8,128)(2,1)S(1)}, u32[]{:S(2)}, u32[]{:S(2)}) async-start(bf16[16,48,128]{2,1,0:T(8,128)(2,1)} %shard_map.73), calls=%async_computation | async-start | bytes 393216 | tf_op jit(solution)/shard_map/all_to_all | solution.py:147
  9.7 1.5 %shard_map.74.doubled_ref = bf16[16,17,32,128]{3,2,1,0:T(8,128)(2,1)S(1)} custom-call(bf16[32,16384]{1,0:T(8,128)(2,1)S(1)} %copy-done.1), custom_call_target="tpu_custom_call" | custom-call | flops 4194304 | bytes 3145728 | tf_op jit(solution)/shard_map/pallas_call | solution.py:157
  11.1 6.7 %all-to-all-done = bf16[16,48,128]{2,1,0:T(8,128)(2,1)S(1)} async-done(((bf16[16,48,128]{2,1,0:T(8,128)(2,1)}), bf16[16,48,128]{2,1,0:T(8,128)(2,1)S(1)}, u32[]{:S(2)}, u32[]{:S(2)}) %all-to-all-start) | async-done | bytes 196640 | tf_op jit(solution)/shard_map/all_to_all | solution.py:147
  17.8 1.9 %shard_map.75 = bf16[16,16,32,128]{3,2,1,0:T(8,128)(2,1)S(1)} custom-call(s32[16,32]{1,0:T(8,128)S(1)} %fusion.2.table_ref, bf16[16,17,32,128]{3,2,1,0:T(8,128)(2,1)S(1)} %shard_map.74.doubled_ref), custom_call_target="tpu_custom_call" | custom-call | tf_op jit(solution)/shard_map/pallas_call | solution.py:167
  19.7 1.3 %copy-done = bf16[16,16,32,128]{3,2,1,0:T(8,128)(2,1)} copy-done((bf16[16,16,32,128]{3,2,1,0:T(8,128)(2,1)}, bf16[16,16,32,128]{3,2,1,0:T(8,128)(2,1)S(1)}, u32[]{:S(2)}) %copy-start) | copy-done | bytes 2097176
  21.0 3.8 %all-to-all-start.1 = ((bf16[16,16,32,128]{3,2,1,0:T(8,128)(2,1)}), bf16[16,16,32,128]{3,2,1,0:T(8,128)(2,1)S(1)}, u32[]{:S(2)}, u32[]{:S(2)}) async-start(bf16[16,16,32,128]{3,2,1,0:T(8,128)(2,1)} %copy-done), calls=%async_computation.1 | async-start | bytes 4194304 | tf_op jit(solution)/shard_map/all_to_all | solution.py:147
  24.9 1.3 %collective-permute-start = (bf16[16,32,128]{2,1,0:T(8,128)(2,1)S(1)}, bf16[16,32,128]{2,1,0:T(8,128)(2,1)S(1)}, u32[]{:S(2)}, u32[]{:S(2)}) collective-permute-start(bf16[16,32,128]{2,1,0:T(8,128)(2,1)S(1)} %slice_select_fusion), channel_id=1, source_target_pairs={{0,16},{1,17},{2,18},{3,19},{4,20},{5,21},{6,22},{7,23},{8,24},{9,... | collective-permute-start | bytes 393224 | tf_op jit(solution)/shard_map/ppermute | solution.py:180
  26.2 1.0 %collective-permute-done = bf16[16,32,128]{2,1,0:T(8,128)(2,1)S(1)} collective-permute-done((bf16[16,32,128]{2,1,0:T(8,128)(2,1)S(1)}, bf16[16,32,128]{2,1,0:T(8,128)(2,1)S(1)}, u32[]{:S(2)}, u32[]{:S(2)}) %collective-permute-start) | collective-permute-done | bytes 131104 | tf_op jit(solution)/shard_map/ppermute | solution.py:180
  27.2 1.8 %collective-permute-start.1 = (bf16[16,32,128]{2,1,0:T(8,128)(2,1)S(1)}, bf16[16,32,128]{2,1,0:T(8,128)(2,1)S(1)}, u32[]{:S(2)}, u32[]{:S(2)}) collective-permute-start(bf16[16,32,128]{2,1,0:T(8,128)(2,1)S(1)} %fusion.3), channel_id=1, source_target_pairs={{0,32},{16,48},{1,33},{17,49},{2,34},{18,50},{3,35},{19,51},{4,36}... | collective-permute-start | bytes 393224 | tf_op jit(solution)/shard_map/ppermute | solution.py:180
  29.1 0.7 dynamic-slice_subtract_fusion
  29.8 2.2 %collective-permute-done.1 = bf16[16,32,128]{2,1,0:T(8,128)(2,1)S(1)} collective-permute-done((bf16[16,32,128]{2,1,0:T(8,128)(2,1)S(1)}, bf16[16,32,128]{2,1,0:T(8,128)(2,1)S(1)}, u32[]{:S(2)}, u32[]{:S(2)}) %collective-permute-start.1) | collective-permute-done | bytes 131104 | tf_op jit(solution)/shard_map/ppermute | solution.py:180
  32.1 1.3 %collective-permute-start.2 = (bf16[16,32,128]{2,1,0:T(8,128)(2,1)S(1)}, bf16[16,32,128]{2,1,0:T(8,128)(2,1)S(1)}, u32[]{:S(2)}, u32[]{:S(2)}) collective-permute-start(bf16[16,32,128]{2,1,0:T(8,128)(2,1)S(1)} %add.16), channel_id=1, source_target_pairs={{0,64},{16,80},{32,96},{48,112},{1,65},{17,81},{33,97},{49,113},{2... | collective-permute-start | bytes 393224 | tf_op jit(solution)/shard_map/ppermute | solution.py:180
  33.4 2.5 %collective-permute-done.2 = bf16[16,32,128]{2,1,0:T(8,128)(2,1)S(1)} collective-permute-done((bf16[16,32,128]{2,1,0:T(8,128)(2,1)S(1)}, bf16[16,32,128]{2,1,0:T(8,128)(2,1)S(1)}, u32[]{:S(2)}, u32[]{:S(2)}) %collective-permute-start.2) | collective-permute-done | bytes 131104 | tf_op jit(solution)/shard_map/ppermute | solution.py:180
  36.2 17.4 %all-to-all-done.1.slab_ref = bf16[16,16,32,128]{3,2,1,0:T(8,128)(2,1)S(1)} async-done(((bf16[16,16,32,128]{3,2,1,0:T(8,128)(2,1)}), bf16[16,16,32,128]{3,2,1,0:T(8,128)(2,1)S(1)}, u32[]{:S(2)}, u32[]{:S(2)}) %all-to-all-start.1) | async-done | bytes 2097184 | tf_op jit(solution)/shard_map/all_to_all | solution.py:147
  53.6 1.4 %copy-done.2 = bf16[32,3,64,128]{3,2,1,0:T(8,128)(2,1)S(1)} copy-done((bf16[32,3,64,128]{3,2,1,0:T(8,128)(2,1)S(1)}, bf16[32,3,64,128]{3,2,1,0:T(8,128)(2,1)}, u32[]{:S(2)}) %copy-start.2) | copy-done | bytes 1572888
  55.0 1.4 %copy-done.3 = bf16[32,3,64,128]{3,2,1,0:T(8,128)(2,1)S(1)} copy-done((bf16[32,3,64,128]{3,2,1,0:T(8,128)(2,1)S(1)}, bf16[32,3,64,128]{3,2,1,0:T(8,128)(2,1)}, u32[]{:S(2)}) %copy-start.3) | copy-done | bytes 1572888
  56.4 3.1 %shard_map.76 = bf16[16,16,128]{2,1,0:T(8,128)(2,1)} custom-call(bf16[16,16,32,128]{3,2,1,0:T(8,128)(2,1)S(1)} %all-to-all-done.1.slab_ref, bf16[256,512]{1,0:T(8,128)(2,1)S(1)} %pad_maximum_fusion.weights_ref, bf16[32,3,64,128]{3,2,1,0:T(8,128)(2,1)S(1)} %copy-done.2, bf16[32,3,64,128]{3,2,1,0:T(8,128)(2,1)S(1)} %copy-done.3), custom_call_target="tpu_custom_call" | custom-call | tf_op jit(solution)/shard_map/pallas_call | solution.py:203
  59.5 3.7 %all-to-all-start.2 = ((bf16[16,16,128]{2,1,0:T(8,128)(2,1)}), bf16[16,16,128]{2,1,0:T(8,128)(2,1)S(1)}, u32[]{:S(2)}, u32[]{:S(2)}) async-start(bf16[16,16,128]{2,1,0:T(8,128)(2,1)} %shard_map.76), calls=%async_computation.2 | async-start | bytes 131072 | tf_op jit(solution)/shard_map/all_to_all | solution.py:147
  63.2 0.7 pad_add_fusion.atom_ref
  63.9 2.3 %shard_map.77.hot_ref = bf16[16,128,256]{2,1,0:T(8,128)(2,1)} custom-call(s32[16]{0:T(128)} %owner_ref.3, s32[16,128]{1,0:T(8,128)} %pad_add_fusion.atom_ref), custom_call_target="tpu_custom_call" | custom-call | flops 4194304 | bytes 1048576 | tf_op jit(solution)/shard_map/pallas_call | solution.py:194
  66.2 4.7 %all-to-all-done.2.force_ref = bf16[16,16,128]{2,1,0:T(8,128)(2,1)S(1)} async-done(((bf16[16,16,128]{2,1,0:T(8,128)(2,1)}), bf16[16,16,128]{2,1,0:T(8,128)(2,1)S(1)}, u32[]{:S(2)}, u32[]{:S(2)}) %all-to-all-start.2) | async-done | bytes 65568 | tf_op jit(solution)/shard_map/all_to_all | solution.py:147
  70.9 0.6 copy-done.4
  71.5 2.1 %shard_map.78 = f32[3,160]{1,0:T(4,128)} custom-call(bf16[16,16,128]{2,1,0:T(8,128)(2,1)} %copy-done.4, bf16[16,128,256]{2,1,0:T(8,128)(2,1)} %shard_map.77.hot_ref), custom_call_target="tpu_custom_call" | custom-call | tf_op jit(solution)/shard_map/pallas_call | solution.py:218
  (23 shorter events, 0.4 us)
Async XLA Ops:
  0.0 9.6 %copy-start.1 = (bf16[32,16384]{1,0:T(8,128)(2,1)S(1)}, bf16[32,16384]{1,0:T(8,128)(2,1)}, u32[]{:S(2)}) copy-start(bf16[32,16384]{1,0:T(8,128)(2,1)} %slab_ref.1) | copy-start | bytes 3145732
  1.5 16.3 %all-to-all-start = ((bf16[16,48,128]{2,1,0:T(8,128)(2,1)}), bf16[16,48,128]{2,1,0:T(8,128)(2,1)S(1)}, u32[]{:S(2)}, u32[]{:S(2)}) async-start(bf16[16,48,128]{2,1,0:T(8,128)(2,1)} %shard_map.73), calls=%async_computation | async-start | bytes 393216 | tf_op jit(solution)/shard_map/all_to_all | solution.py:147
  19.7 1.3 %copy-start = (bf16[16,16,32,128]{3,2,1,0:T(8,128)(2,1)}, bf16[16,16,32,128]{3,2,1,0:T(8,128)(2,1)S(1)}, u32[]{:S(2)}) copy-start(bf16[16,16,32,128]{3,2,1,0:T(8,128)(2,1)S(1)} %shard_map.75) | copy-start | bytes 6291460
  21.0 8.0 %copy-start.5 = (s32[512]{0:T(512)S(1)}, s32[512]{0:T(512)}, u32[]{:S(2)}) copy-start(s32[512]{0:T(512)} %param.8) | copy-start | bytes 6148
  21.0 12.4 %copy-start.6 = (f32[512]{0:T(512)S(1)}, f32[512]{0:T(512)}, u32[]{:S(2)}) copy-start(f32[512]{0:T(512)} %param.9) | copy-start | bytes 6148
  21.0 32.5 %all-to-all-start.1 = ((bf16[16,16,32,128]{3,2,1,0:T(8,128)(2,1)}), bf16[16,16,32,128]{3,2,1,0:T(8,128)(2,1)S(1)}, u32[]{:S(2)}, u32[]{:S(2)}) async-start(bf16[16,16,32,128]{3,2,1,0:T(8,128)(2,1)} %copy-done), calls=%async_computation.1 | async-start | bytes 4194304 | tf_op jit(solution)/shard_map/all_to_all | solution.py:147
  24.9 2.3 %collective-permute-start = (bf16[16,32,128]{2,1,0:T(8,128)(2,1)S(1)}, bf16[16,32,128]{2,1,0:T(8,128)(2,1)S(1)}, u32[]{:S(2)}, u32[]{:S(2)}) collective-permute-start(bf16[16,32,128]{2,1,0:T(8,128)(2,1)S(1)} %slice_select_fusion), channel_id=1, source_target_pairs={{0,16},{1,17},{2,18},{3,19},{4,20},{5,21},{6,22},{7,23},{8,24},{9,... | collective-permute-start | bytes 393224 | tf_op jit(solution)/shard_map/ppermute | solution.py:180
  27.2 4.8 %collective-permute-start.1 = (bf16[16,32,128]{2,1,0:T(8,128)(2,1)S(1)}, bf16[16,32,128]{2,1,0:T(8,128)(2,1)S(1)}, u32[]{:S(2)}, u32[]{:S(2)}) collective-permute-start(bf16[16,32,128]{2,1,0:T(8,128)(2,1)S(1)} %fusion.3), channel_id=1, source_target_pairs={{0,32},{16,48},{1,33},{17,49},{2,34},{18,50},{3,35},{19,51},{4,36}... | collective-permute-start | bytes 393224 | tf_op jit(solution)/shard_map/ppermute | solution.py:180
  32.1 3.8 %collective-permute-start.2 = (bf16[16,32,128]{2,1,0:T(8,128)(2,1)S(1)}, bf16[16,32,128]{2,1,0:T(8,128)(2,1)S(1)}, u32[]{:S(2)}, u32[]{:S(2)}) collective-permute-start(bf16[16,32,128]{2,1,0:T(8,128)(2,1)S(1)} %add.16), channel_id=1, source_target_pairs={{0,64},{16,80},{32,96},{48,112},{1,65},{17,81},{33,97},{49,113},{2... | collective-permute-start | bytes 393224 | tf_op jit(solution)/shard_map/ppermute | solution.py:180
  53.6 1.4 %copy-start.2 = (bf16[32,3,64,128]{3,2,1,0:T(8,128)(2,1)S(1)}, bf16[32,3,64,128]{3,2,1,0:T(8,128)(2,1)}, u32[]{:S(2)}) copy-start(bf16[32,3,64,128]{3,2,1,0:T(8,128)(2,1)} %ham_hbm.1) | copy-start | bytes 4718596
  55.0 1.4 %copy-start.3 = (bf16[32,3,64,128]{3,2,1,0:T(8,128)(2,1)S(1)}, bf16[32,3,64,128]{3,2,1,0:T(8,128)(2,1)}, u32[]{:S(2)}) copy-start(bf16[32,3,64,128]{3,2,1,0:T(8,128)(2,1)} %margin_hbm.1) | copy-start | bytes 4718596
  59.5 11.4 %all-to-all-start.2 = ((bf16[16,16,128]{2,1,0:T(8,128)(2,1)}), bf16[16,16,128]{2,1,0:T(8,128)(2,1)S(1)}, u32[]{:S(2)}, u32[]{:S(2)}) async-start(bf16[16,16,128]{2,1,0:T(8,128)(2,1)} %shard_map.76), calls=%async_computation.2 | async-start | bytes 131072 | tf_op jit(solution)/shard_map/all_to_all | solution.py:147
  70.9 0.6 copy-start.4

commit v2 on v1

--- a/solution.py
+++ b/solution.py
@@ -28,12 +28,41 @@
     return jnp.where(rank == 0, first, second)
 
 
-def announce_kernel(owner_ref, panel_ref, out_ref):
-    columns, _, width = out_ref.shape
-    states = panel_ref.shape[0]
-    out_ref[:, :states, :] = jnp.broadcast_to(panel_ref[...][None], (columns, states, width))
-    table = slots_of(owner_ref, columns, owner_ref.shape[0], (16, width))
-    out_ref[:, states:, :] = jnp.broadcast_to(table.astype(F32).astype(BF16)[None], (columns, 16, width))
+def announce_kernel(owner_ref, slab_hbm, out_hbm, own_ref, tile_ref, sems):
+    columns, states, width = tile_ref.shape[0], own_ref.shape[0], tile_ref.shape[2]
+    blocks = owner_ref.shape[0]
+    half = width // 2
+    mine = lax.axis_index("col") * (blocks * half)
+    own = pltpu.make_async_copy(slab_hbm.at[:, pl.ds(pl.multiple_of(mine, width), blocks * half)], own_ref, sems.at[columns])
+    own.start()
+    panels = []
+    for o in range(columns):
+        panels.append(pltpu.make_async_copy(slab_hbm.at[:, pl.ds(0, width)], out_hbm.at[o, pl.ds(0, states), :], sems.at[o]))
+        panels[-1].start()
+    rows = tile_ref.shape[1]
+    table = slots_of(owner_ref, columns, blocks, (rows - states, width))
+    tile_ref[:, states:, :] = jnp.broadcast_to(table.astype(F32).astype(BF16)[None], (columns, rows - states, width))
+    tile_ref[:, :states, :] = jnp.zeros((columns, states, width), BF16)
+    low = lax.broadcasted_iota(jnp.int32, (states, width), 1) < half
+    own.wait()
+    for b in range(blocks):
+        o = owner_ref[b]
+        rank = jnp.int32(0)
+        for earlier in range(b):
+            rank = rank + (owner_ref[earlier] == o).astype(jnp.int32)
+        tile = own_ref[:, (b // 2) * width : (b // 2 + 1) * width].astype(F32)
+        turned = pltpu.roll(tile, half, 1)
+        block = jnp.where(low == (b % 2 == 0), tile, turned).astype(BF16)
+
+        @pl.when(o >= 0)
+        def _():
+            tile_ref[o, :states, :] = jnp.where(low == (rank == 0), block, tile_ref[o, :states, :])
+
+    rest = pltpu.make_async_copy(tile_ref, out_hbm.at[:, pl.ds(states, rows), :], sems.at[columns + 1])
+    rest.start()
+    for copy in panels:
+        copy.wait()
+    rest.wait()
 
 
 def double_kernel(slab_ref, out_ref):
@@ -54,50 +83,70 @@
     lax.fori_loop(0, columns, home, 0)
 
 
-def pack_kernel(table_ref, doubled_ref, out_ref):
+def pack_kernel(table_ref, doubled_ref, out_hbm, out_ref, sems):
     columns, homes, states, width = out_ref.shape
+    me = lax.axis_index("col")
     low = lax.broadcasted_iota(jnp.int32, (states, width), 1) < width // 2
-
-    def home(c, carry):
-        for o in range(columns):
+    copies = [pltpu.make_async_copy(out_ref.at[o], out_hbm.at[o], sems.at[o]) for o in range(columns)]
+    for o in range(columns):
+        for j in range(homes):
+            c = j + (j >= me).astype(jnp.int32)
             left = doubled_ref[c, table_ref[c, 2 * o]]
             right = doubled_ref[c, table_ref[c, 2 * o + 1]]
-            out_ref[o, c] = jnp.where(low, left, right)
-        return carry
-
-    lax.fori_loop(0, homes, home, 0)
-
-
-def owner_kernel(slab_ref, weights_ref, ham_hbm, margin_hbm, out_ref, ham_ref, margin_ref, density_ref, sems):
-    chunks, homes, states, width = slab_ref.shape
+            out_ref[o, j] = jnp.where(low, left, right)
+        copies[o].start()
+    for copy in copies:
+        copy.wait()
+
+
+def owner_kernel(slab_ref, heard_ref, weights_ref, ham_hbm, margin_hbm, out_ref, ham_ref, margin_ref, density_ref, sems):
+    chunks, _, states, width = slab_ref.shape
+    homes = chunks
     half = width // 2
-    copy_ham = pltpu.make_async_copy(ham_hbm, ham_ref, sems.at[0])
-    copy_margin = pltpu.make_async_copy(margin_hbm, margin_ref, sems.at[1])
-    copy_ham.start()
-    copy_margin.start()
-    for c in range(homes):
-        pair = slab_ref[:, c].reshape(chunks * states, width)
-        density_ref[c] = jnp.dot(weights_ref[...], pair, preferred_element_type=F32).astype(BF16)
-    copy_ham.wait()
-    copy_margin.wait()
+    parts = sems.shape[0]
+    share = 2 * homes // parts
+    copies = []
+    for p in range(parts):
+        here = pl.ds(p * share, share)
+        copies.append(
+            [
+                pltpu.make_async_copy(ham_hbm.at[here], ham_ref.at[here], sems.at[p, 0]),
+                pltpu.make_async_copy(margin_hbm.at[here], margin_ref.at[here], sems.at[p, 1]),
+            ]
+        )
+        for copy in copies[p]:
+            copy.start()
+
+    def pair_of(c):
+        pieces = []
+        for d in range(chunks):
+            pieces.append(heard_ref[c, states : 2 * states, :] if d == c else slab_ref[d, c - (c > d)])
+        return jnp.concatenate(pieces, axis=0)
+
+    for c in range(0, homes, 2):
+        two = jnp.concatenate([pair_of(c), pair_of(c + 1)], axis=1)
+        density = jnp.dot(weights_ref[...], two, preferred_element_type=F32).astype(BF16)
+        density_ref[:, c * width : (c + 2) * width] = density
     row = lax.broadcasted_iota(jnp.int32, (half, width), 0)
     lane = lax.broadcasted_iota(jnp.int32, (half, width), 1)
     masks = [lane == row + half * k for k in range(2)]
+    slim = lax.broadcasted_iota(jnp.int32, (8, width), 0)
     for c in range(homes):
+        if 2 * c % share == 0:
+            for copy in copies[2 * c // share]:
+                copy.wait()
         change = jnp.concatenate(
             [ham_ref[2 * c : 2 * c + 2].reshape(6 * half, width), margin_ref[2 * c : 2 * c + 2].reshape(6 * half, width)],
             axis=1,
         )
-        product = jnp.dot(change, density_ref[c], preferred_element_type=F32)
+        product = jnp.dot(change, density_ref[:, c * width : (c + 1) * width], preferred_element_type=F32)
         product = product.reshape(2, 3, half, width)
-        parts = []
+        force = jnp.zeros((8, width), F32)
         for x in range(3):
             kept = jnp.where(masks[0], product[0, x], 0.0) + jnp.where(masks[1], product[1, x], 0.0)
-            parts.append(jnp.sum(kept, axis=0, keepdims=True))
-        force = jnp.concatenate(parts + [jnp.zeros((5, width), F32)], axis=0)
-        high = force.astype(BF16)
-        low = (force - high.astype(F32)).astype(BF16)
-        out_ref[c] = jnp.concatenate([high.astype(F32), low.astype(F32)], axis=0).astype(BF16)
+            force = jnp.where(slim == x, jnp.sum(kept, axis=0, keepdims=True), force)
+        high = force.astype(BF16).astype(F32)
+        out_ref[c] = jnp.concatenate([high, force - high], axis=0).astype(BF16)
 
 
 def hot_kernel(owner_ref, atom_ref, out_ref, rows_ref):
@@ -146,12 +195,18 @@
     def swap(x):
         return lax.all_to_all(x, "col", split_axis=0, concat_axis=0, tiled=True)
 
+    rows_heard = 2 * states + 16
     announced = pl.pallas_call(
         announce_kernel,
-        grid=(1,),
-        in_specs=[whole(SMEM), pl.BlockSpec((states, width), lambda i: (0, 0))],
-        out_specs=pl.BlockSpec((columns, states + 16, width), lambda i: (0, 0, 0)),
-        out_shape=jax.ShapeDtypeStruct((columns, states + 16, width), BF16),
+        in_specs=[whole(SMEM), whole(pltpu.HBM)],
+        out_specs=whole(pltpu.HBM),
+        out_shape=jax.ShapeDtypeStruct((columns, rows_heard, width), BF16),
+        scratch_shapes=[
+            pltpu.VMEM((states, blocks * block_rows), BF16),
+            pltpu.VMEM((columns, states + 16, width), BF16),
+            pltpu.SemaphoreType.DMA((columns + 2,)),
+        ],
+        compiler_params=pltpu.CompilerParams(vmem_limit_bytes=4 << 20),
     )(tile_owner, eigvec_slab)
     heard = swap(announced)
     doubled = pl.pallas_call(
@@ -163,12 +218,14 @@
         compiler_params=pltpu.CompilerParams(vmem_limit_bytes=16 << 20),
     )(eigvec_slab)
 
-    table = heard[:, states, : 2 * columns].astype(jnp.int32)
+    table = heard[:, 2 * states, : 2 * columns].astype(jnp.int32)
+    packed_shape = (columns, columns - 1, states, width)
     packed = pl.pallas_call(
         pack_kernel,
         in_specs=[whole(SMEM), whole()],
-        out_specs=whole(),
-        out_shape=jax.ShapeDtypeStruct((columns, columns, states, width), BF16),
+        out_specs=whole(pltpu.HBM),
+        out_shape=jax.ShapeDtypeStruct(packed_shape, BF16),
+        scratch_shapes=[pltpu.VMEM(packed_shape, BF16), pltpu.SemaphoreType.DMA((columns,))],
         compiler_params=pltpu.CompilerParams(vmem_limit_bytes=16 << 20),
     )(table, doubled)
     slabs = swap(packed)
@@ -198,21 +255,22 @@
         out_shape=jax.ShapeDtypeStruct((columns, width, atoms_padded), BF16),
         scratch_shapes=[pltpu.VMEM((columns, width), jnp.int32)],
         cost_estimate=pl.CostEstimate(flops=4 << 20, bytes_accessed=1 << 20, transcendentals=0),
+        compiler_params=pltpu.CompilerParams(vmem_limit_bytes=8 << 20),
     )(tile_owner, atom)
 
     force = pl.pallas_call(
         owner_kernel,
-        in_specs=[whole(), whole(), whole(pl.ANY), whole(pl.ANY)],
+        in_specs=[whole(), whole(), whole(), whole(pltpu.HBM), whole(pltpu.HBM)],
         out_specs=whole(),
         out_shape=jax.ShapeDtypeStruct((columns, 16, width), BF16),
         scratch_shapes=[
             pltpu.VMEM(hamiltonian_change.shape, BF16),
             pltpu.VMEM(margin_change.shape, BF16),
-            pltpu.VMEM((columns, 2 * width, width), BF16),
-            pltpu.SemaphoreType.DMA((2,)),
+            pltpu.VMEM((2 * width, columns * width), BF16),
+            pltpu.SemaphoreType.DMA((4, 2)),
         ],
         compiler_params=pltpu.CompilerParams(vmem_limit_bytes=32 << 20),
-    )(slabs, weights, hamiltonian_change, margin_change)
+    )(slabs, heard, weights, hamiltonian_change, margin_change)
 
     returned = swap(force)
     return pl.pallas_call(
@@ -220,6 +278,7 @@
         in_specs=[whole(), whole()],
         out_specs=whole(),
         out_shape=jax.ShapeDtypeStruct((3, ATOMS_DEV), F32),
+        compiler_params=pltpu.CompilerParams(vmem_limit_bytes=8 << 20),
     )(returned, hot)
 
 

time: 74.1 us -> 80.2 us (1.082)
  waiting for transfers between devices: 34.4 us -> 26.7 us
  other arithmetic: 1.57 us -> 8.32 us
  Pallas kernels: 12.3 us -> 15.6 us
  local copies, waits for them, and re-layouts: 4.98 us -> 8.03 us
    all_to_all x3, waiting for transfers between devices: 28.8 us -> 22 us  [swap(): return lax.all_to_all(x, 'col', split_axis=0, concat_axis=0, tiled=True)]
    pallas_call x2, Pallas kernels: 4.59 us -> 7.57 us  [the longest x1 4.81 us: per_device(): pl.pallas_call(owner_kernel, in_specs=[whole(), whole(), whole(), whole(p...]
    pallas_call x1, Pallas kernels: 1.86 us -> 4.6 us  [per_device(): pl.pallas_call(pack_kernel, in_specs=[whole(SMEM), whole()], out_specs=wh...]
    add x3, other arithmetic: 0.09 us -> 2.61 us  [per_device(): panel + lax.ppermute(panel, 'row', [(i, i + reach) for i in range(reach)])]
    convert_element_type x1, local copies, waits for them, and re-layouts: 0.13 us -> 1.8 us  [per_device(): panel_t = panel.reshape(columns * states, width).T.astype(F32)]
    unnamed x14 -> x20, local copies, waits for them, and re-layouts: 4.77 us -> 6.16 us
    pallas_call x1, Pallas kernels: 2.11 us -> 0.85 us  [per_device(): pl.pallas_call(gather_kernel, in_specs=[whole(), whole()], out_specs=whol...]
    pallas_call x1, Pallas kernels: 2.3 us -> 1.16 us  [per_device(): pl.pallas_call(hot_kernel, in_specs=[whole(SMEM), whole()], out_specs=who...]
  transfers between devices with their start and end apart: 6 -> 6, of which waited for: 6 -> 6; matrix products, arithmetic and copies ran while one was open for 2% -> 12% of each run, Pallas kernels for 5% -> 3%
where the time goes in v2:
time: 80.2 us; the launch traced here: 79.5 us
  waiting for transfers between devices  26.7 us (33%)
  starting transfers between devices  20.6 us (26%)
  Pallas kernels  15.6 us (19%)
  other arithmetic  8.32 us (10%)
  local copies, waits for them, and re-layouts  8.03 us (10%)
    all_to_all x3, waiting for transfers between devices, swap(): return lax.all_to_all(x, 'col', split_axis=0, concat_axis=0, tiled=True)  22 us
    all_to_all x3, starting transfers between devices, swap(): return lax.all_to_all(x, 'col', split_axis=0, concat_axis=0, tiled=True)  15.6 us
    unnamed x20, local copies, waits for them, and re-layouts  6.16 us
    ppermute x3, starting transfers between devices, per_device(): lax.ppermute(panel, 'row', [(i, i + reach) for i in range(reach)])  5.07 us
    pallas_call x1, Pallas kernels, per_device(): pl.pallas_call(owner_kernel, in_specs=[whole(), whole(), whole(), whole(p...  4.81 us
    ppermute x3, waiting for transfers between devices, per_device(): lax.ppermute(panel, 'row', [(i, i + reach) for i in range(reach)])  4.66 us
    pallas_call x1, Pallas kernels, per_device(): pl.pallas_call(pack_kernel, in_specs=[whole(SMEM), whole()], out_specs=wh...  4.6 us
    pallas_call x1, Pallas kernels, per_device(): pl.pallas_call(announce_kernel, in_specs=[whole(SMEM), whole(pltpu.HBM)],...  2.76 us
  transfers between devices with their start and end apart: 6, of which 6 were waited for; matrix products, arithmetic and copies ran while one was open for 12% of the time, Pallas kernels for 3%

profile of v2, /device:TPU:0, one launch (start us, length us, event | category | flops | bytes accessed | tf_op | source)
XLA Modules:
  0.0 79.5 jit_solution(259925610080669031)
XLA Ops:
  0.0 1.2 %copy-done.1 = bf16[32,16384]{1,0:T(8,128)(2,1)S(1)} copy-done((bf16[32,16384]{1,0:T(8,128)(2,1)S(1)}, bf16[32,16384]{1,0:T(8,128)(2,1)}, u32[]{:S(2)}) %copy-start.1) | copy-done | bytes 1048600
  1.9 2.8 %shard_map.73 = bf16[16,80,128]{2,1,0:T(8,128)(2,1)} custom-call(s32[16]{0:T(128)S(1)} %copy-done.7, bf16[32,16384]{1,0:T(8,128)(2,1)S(1)} %copy-done.1), custom_call_target="tpu_custom_call" | custom-call | tf_op jit(solution)/shard_map/pallas_call | solution.py:199
  4.7 8.2 %all-to-all-start = ((bf16[16,80,128]{2,1,0:T(8,128)(2,1)}), bf16[16,80,128]{2,1,0:T(8,128)(2,1)}, u32[]{:S(2)}, u32[]{:S(2)}) async-start(bf16[16,80,128]{2,1,0:T(8,128)(2,1)} %shard_map.73), calls=%async_computation | async-start | bytes 655360 | tf_op jit(solution)/shard_map/all_to_all | solution.py:196
  12.9 1.5 %shard_map.74.doubled_ref = bf16[16,17,32,128]{3,2,1,0:T(8,128)(2,1)S(1)} custom-call(bf16[32,16384]{1,0:T(8,128)(2,1)S(1)} %copy-done.2), custom_call_target="tpu_custom_call" | custom-call | flops 4194304 | bytes 3145728 | tf_op jit(solution)/shard_map/pallas_call | solution.py:212
  14.3 7.7 %all-to-all-done.heard_ref = bf16[16,80,128]{2,1,0:T(8,128)(2,1)} async-done(((bf16[16,80,128]{2,1,0:T(8,128)(2,1)}), bf16[16,80,128]{2,1,0:T(8,128)(2,1)}, u32[]{:S(2)}, u32[]{:S(2)}) %all-to-all-start) | async-done | bytes 327712 | tf_op jit(solution)/shard_map/all_to_all | solution.py:196
  22.8 4.6 %shard_map.75 = bf16[16,15,32,128]{3,2,1,0:T(8,128)(2,1)S(1)} custom-call(s32[16,32]{1,0:T(8,128)S(1)} %bitcast.8, bf16[16,17,32,128]{3,2,1,0:T(8,128)(2,1)S(1)} %shard_map.74.doubled_ref), custom_call_target="tpu_custom_call" | custom-call | tf_op jit(solution)/shard_map/pallas_call | solution.py:223
  27.4 1.3 %copy-done = bf16[16,15,32,128]{3,2,1,0:T(8,128)(2,1)} copy-done((bf16[16,15,32,128]{3,2,1,0:T(8,128)(2,1)}, bf16[16,15,32,128]{3,2,1,0:T(8,128)(2,1)S(1)}, u32[]{:S(2)}) %copy-start) | copy-done | bytes 1966104
  28.7 3.8 %all-to-all-start.1 = ((bf16[16,15,32,128]{3,2,1,0:T(8,128)(2,1)}), bf16[16,15,32,128]{3,2,1,0:T(8,128)(2,1)S(1)}, u32[]{:S(2)}, u32[]{:S(2)}) async-start(bf16[16,15,32,128]{3,2,1,0:T(8,128)(2,1)} %copy-done), calls=%async_computation.1 | async-start | bytes 3932160 | tf_op jit(solution)/shard_map/all_to_all | solution.py:196
  32.6 1.0 %slice_select_fusion = bf16[16,32,128]{2,1,0:T(8,128)(2,1)S(1)} fusion(bf16[16,80,128]{2,1,0:T(8,128)(2,1)} %all-to-all-done.heard_ref, pred[]{:T(512)S(6)} %eq.3), kind=kLoop, calls=%fused_computation.5 | loop fusion | flops 65536 | bytes 262145 | tf_op jit(solution)/shard_map/jit(_where)/select_n | solution.py:234
  33.6 1.3 %collective-permute-start = (bf16[16,32,128]{2,1,0:T(8,128)(2,1)S(1)}, bf16[16,32,128]{2,1,0:T(8,128)(2,1)S(1)}, u32[]{:S(2)}, u32[]{:S(2)}) collective-permute-start(bf16[16,32,128]{2,1,0:T(8,128)(2,1)S(1)} %slice_select_fusion), channel_id=1, source_target_pairs={{0,16},{1,17},{2,18},{3,19},{4,20},{5,21},{6,22},{7,23},{8,24},{9,... | collective-permute-start | bytes 393224 | tf_op jit(solution)/shard_map/ppermute | solution.py:237
  35.9 1.6 %fusion.2 = bf16[16,32,128]{2,1,0:T(8,128)(2,1)} fusion(bf16[16,32,128]{2,1,0:T(8,128)(2,1)S(1)} %collective-permute-done, bf16[16,80,128]{2,1,0:T(8,128)(2,1)} %all-to-all-done.heard_ref, pred[]{:T(512)S(6)} %eq.3), kind=kLoop, calls=%fused_computation.11 | loop fusion | flops 131072 | bytes 393217 | tf_op jit(solution)/shard_map/add | solution.py:237
  37.5 2.5 %collective-permute-start.1 = (bf16[16,32,128]{2,1,0:T(8,128)(2,1)}, bf16[16,32,128]{2,1,0:T(8,128)(2,1)}, u32[]{:S(2)}, u32[]{:S(2)}) collective-permute-start(bf16[16,32,128]{2,1,0:T(8,128)(2,1)} %fusion.2), channel_id=1, source_target_pairs={{0,32},{16,48},{1,33},{17,49},{2,34},{18,50},{3,35},{19,51},{4,36}... | collective-permute-start | bytes 393224 | tf_op jit(solution)/shard_map/ppermute | solution.py:237
  40.7 1.9 %collective-permute-done.1 = bf16[16,32,128]{2,1,0:T(8,128)(2,1)} collective-permute-done((bf16[16,32,128]{2,1,0:T(8,128)(2,1)}, bf16[16,32,128]{2,1,0:T(8,128)(2,1)}, u32[]{:S(2)}, u32[]{:S(2)}) %collective-permute-start.1) | collective-permute-done | bytes 131104 | tf_op jit(solution)/shard_map/ppermute | solution.py:237
  42.6 1.0 %add.16 = bf16[16,32,128]{2,1,0:T(8,128)(2,1)S(1)} add(bf16[16,32,128]{2,1,0:T(8,128)(2,1)} %fusion.2, bf16[16,32,128]{2,1,0:T(8,128)(2,1)} %collective-permute-done.1) | non-fusion elementwise | flops 65536 | bytes 393216 | tf_op jit(solution)/shard_map/add | solution.py:237
  43.6 1.3 %collective-permute-start.2 = (bf16[16,32,128]{2,1,0:T(8,128)(2,1)S(1)}, bf16[16,32,128]{2,1,0:T(8,128)(2,1)S(1)}, u32[]{:S(2)}, u32[]{:S(2)}) collective-permute-start(bf16[16,32,128]{2,1,0:T(8,128)(2,1)S(1)} %add.16), channel_id=1, source_target_pairs={{0,64},{16,80},{32,96},{48,112},{1,65},{17,81},{33,97},{49,113},{2... | collective-permute-start | bytes 393224 | tf_op jit(solution)/shard_map/ppermute | solution.py:237
  45.6 1.8 %collective-permute-done.2 = bf16[16,32,128]{2,1,0:T(8,128)(2,1)S(1)} collective-permute-done((bf16[16,32,128]{2,1,0:T(8,128)(2,1)S(1)}, bf16[16,32,128]{2,1,0:T(8,128)(2,1)S(1)}, u32[]{:S(2)}, u32[]{:S(2)}) %collective-permute-start.2) | collective-permute-done | bytes 131104 | tf_op jit(solution)/shard_map/ppermute | solution.py:237
  48.2 1.8 %copy.9 = f32[512,128]{0,1:T(8,128)} copy(f32[512,128]{1,0:T(8,128)} %bitcast_convert_fusion) | data formatting | bytes 524288 | tf_op jit(solution)/shard_map/convert_element_type | solution.py:241
  50.0 1.0 %fusion = (bf16[128,512]{1,0:T(8,128)(2,1)S(1)}, bf16[128,512]{1,0:T(8,128)(2,1)S(1)}) fusion(f32[512,128]{0,1:T(8,128)} %copy.9, f32[512]{0:T(512)S(1)} %convert_element_type.31, f32[512]{0:T(512)S(1)} %multiply_negate_fusion), kind=kLoop, calls=%fused_computation.3 | loop fusion | flops 262144 | bytes 528384 | tf_op jit(solution)/shard_map/convert_element_type | solution.py:243
  51.7 7.9 %all-to-all-done.1.slab_ref = bf16[16,15,32,128]{3,2,1,0:T(8,128)(2,1)S(1)} async-done(((bf16[16,15,32,128]{3,2,1,0:T(8,128)(2,1)}), bf16[16,15,32,128]{3,2,1,0:T(8,128)(2,1)S(1)}, u32[]{:S(2)}, u32[]{:S(2)}) %all-to-all-start.1) | async-done | bytes 1966112 | tf_op jit(solution)/shard_map/all_to_all | solution.py:196
  59.6 1.4 %copy-done.4 = bf16[32,3,64,128]{3,2,1,0:T(8,128)(2,1)S(1)} copy-done((bf16[32,3,64,128]{3,2,1,0:T(8,128)(2,1)S(1)}, bf16[32,3,64,128]{3,2,1,0:T(8,128)(2,1)}, u32[]{:S(2)}) %copy-start.4) | copy-done | bytes 1572888
  62.0 4.8 %shard_map.76 = bf16[16,16,128]{2,1,0:T(8,128)(2,1)S(1)} custom-call(bf16[16,15,32,128]{3,2,1,0:T(8,128)(2,1)S(1)} %all-to-all-done.1.slab_ref, bf16[16,80,128]{2,1,0:T(8,128)(2,1)} %all-to-all-done.heard_ref, bf16[256,512]{1,0:T(8,128)(2,1)S(1)} %copy-done.5, bf16[32,3,64,128]{3,2,1,0:T(8,128)(2,1)S(1)} %copy-done.3, bf16[32,3,64,128]{3,2,1,0:T(8,128)(2,1)S(1)} %copy-done.4), custom_call_target="tpu_custom_call" | custom-call | tf_op jit(solution)/shard_map/pallas_call | solution.py:261
  67.4 3.5 %all-to-all-start.2 = ((bf16[16,16,128]{2,1,0:T(8,128)(2,1)}), bf16[16,16,128]{2,1,0:T(8,128)(2,1)S(1)}, u32[]{:S(2)}, u32[]{:S(2)}) async-start(bf16[16,16,128]{2,1,0:T(8,128)(2,1)} %copy-done.6), calls=%async_computation.2 | async-start | bytes 131072 | tf_op jit(solution)/shard_map/all_to_all | solution.py:196
  71.0 1.2 %shard_map.77.hot_ref = bf16[16,128,256]{2,1,0:T(8,128)(2,1)S(1)} custom-call(s32[16]{0:T(128)S(1)} %copy-done.8, s32[16,128]{1,0:T(8,128)S(1)} %pad_add_fusion.atom_ref), custom_call_target="tpu_custom_call" | custom-call | flops 4194304 | bytes 1048576 | tf_op jit(solution)/shard_map/pallas_call | solution.py:251
  72.2 6.4 %all-to-all-done.2.force_ref = bf16[16,16,128]{2,1,0:T(8,128)(2,1)S(1)} async-done(((bf16[16,16,128]{2,1,0:T(8,128)(2,1)}), bf16[16,16,128]{2,1,0:T(8,128)(2,1)S(1)}, u32[]{:S(2)}, u32[]{:S(2)}) %all-to-all-start.2) | async-done | bytes 65568 | tf_op jit(solution)/shard_map/all_to_all | solution.py:196
  (28 shorter events, 7.9 us)
Async XLA Ops:
  0.0 1.2 %copy-start.1 = (bf16[32,16384]{1,0:T(8,128)(2,1)S(1)}, bf16[32,16384]{1,0:T(8,128)(2,1)}, u32[]{:S(2)}) copy-start(bf16[32,16384]{1,0:T(8,128)(2,1)} %slab_ref.1) | copy-start | bytes 3145732
  1.2 0.7 copy-start.7
  1.9 11.0 %copy-start.2 = (bf16[32,16384]{1,0:T(8,128)(2,1)S(1)}, bf16[32,16384]{1,0:T(8,128)(2,1)}, u32[]{:S(2)}) copy-start(bf16[32,16384]{1,0:T(8,128)(2,1)} %slab_ref.1) | copy-start | bytes 3145732
  4.7 17.4 %all-to-all-start = ((bf16[16,80,128]{2,1,0:T(8,128)(2,1)}), bf16[16,80,128]{2,1,0:T(8,128)(2,1)}, u32[]{:S(2)}, u32[]{:S(2)}) async-start(bf16[16,80,128]{2,1,0:T(8,128)(2,1)} %shard_map.73), calls=%async_computation | async-start | bytes 655360 | tf_op jit(solution)/shard_map/all_to_all | solution.py:196
  27.4 1.3 %copy-start = (bf16[16,15,32,128]{3,2,1,0:T(8,128)(2,1)}, bf16[16,15,32,128]{3,2,1,0:T(8,128)(2,1)S(1)}, u32[]{:S(2)}) copy-start(bf16[16,15,32,128]{3,2,1,0:T(8,128)(2,1)S(1)} %shard_map.75) | copy-start | bytes 5898244
  28.7 11.2 %copy-start.9 = (s32[512]{0:T(512)S(1)}, s32[512]{0:T(512)}, u32[]{:S(2)}) copy-start(s32[512]{0:T(512)} %param.8) | copy-start | bytes 6148
  28.7 30.9 %all-to-all-start.1 = ((bf16[16,15,32,128]{3,2,1,0:T(8,128)(2,1)}), bf16[16,15,32,128]{3,2,1,0:T(8,128)(2,1)S(1)}, u32[]{:S(2)}, u32[]{:S(2)}) async-start(bf16[16,15,32,128]{3,2,1,0:T(8,128)(2,1)} %copy-done), calls=%async_computation.1 | async-start | bytes 3932160 | tf_op jit(solution)/shard_map/all_to_all | solution.py:196
  32.6 27.0 %copy-start.3 = (bf16[32,3,64,128]{3,2,1,0:T(8,128)(2,1)S(1)}, bf16[32,3,64,128]{3,2,1,0:T(8,128)(2,1)}, u32[]{:S(2)}) copy-start(bf16[32,3,64,128]{3,2,1,0:T(8,128)(2,1)} %ham_hbm.1) | copy-start | bytes 4718596
  33.6 2.3 %collective-permute-start = (bf16[16,32,128]{2,1,0:T(8,128)(2,1)S(1)}, bf16[16,32,128]{2,1,0:T(8,128)(2,1)S(1)}, u32[]{:S(2)}, u32[]{:S(2)}) collective-permute-start(bf16[16,32,128]{2,1,0:T(8,128)(2,1)S(1)} %slice_select_fusion), channel_id=1, source_target_pairs={{0,16},{1,17},{2,18},{3,19},{4,20},{5,21},{6,22},{7,23},{8,24},{9,... | collective-permute-start | bytes 393224 | tf_op jit(solution)/shard_map/ppermute | solution.py:237
  37.5 5.1 %collective-permute-start.1 = (bf16[16,32,128]{2,1,0:T(8,128)(2,1)}, bf16[16,32,128]{2,1,0:T(8,128)(2,1)}, u32[]{:S(2)}, u32[]{:S(2)}) collective-permute-start(bf16[16,32,128]{2,1,0:T(8,128)(2,1)} %fusion.2), channel_id=1, source_target_pairs={{0,32},{16,48},{1,33},{17,49},{2,34},{18,50},{3,35},{19,51},{4,36}... | collective-permute-start | bytes 393224 | tf_op jit(solution)/shard_map/ppermute | solution.py:237
  43.6 3.8 %collective-permute-start.2 = (bf16[16,32,128]{2,1,0:T(8,128)(2,1)S(1)}, bf16[16,32,128]{2,1,0:T(8,128)(2,1)S(1)}, u32[]{:S(2)}, u32[]{:S(2)}) collective-permute-start(bf16[16,32,128]{2,1,0:T(8,128)(2,1)S(1)} %add.16), channel_id=1, source_target_pairs={{0,64},{16,80},{32,96},{48,112},{1,65},{17,81},{33,97},{49,113},{2... | collective-permute-start | bytes 393224 | tf_op jit(solution)/shard_map/ppermute | solution.py:237
  59.6 1.4 %copy-start.4 = (bf16[32,3,64,128]{3,2,1,0:T(8,128)(2,1)S(1)}, bf16[32,3,64,128]{3,2,1,0:T(8,128)(2,1)}, u32[]{:S(2)}) copy-start(bf16[32,3,64,128]{3,2,1,0:T(8,128)(2,1)} %margin_hbm.1) | copy-start | bytes 4718596
  61.0 0.9 %copy-start.5 = (bf16[256,512]{1,0:T(8,128)(2,1)S(1)}, bf16[256,512]{1,0:T(8,128)(2,1)}, u32[]{:S(2)}) copy-start(bf16[256,512]{1,0:T(8,128)(2,1)} %pad_maximum_fusion.weights_ref) | copy-start | bytes 786436
  62.0 9.1 %copy-start.8 = (s32[16]{0:T(128)S(1)}, s32[16]{0:T(128)}, u32[]{:S(2)}) copy-start(s32[16]{0:T(128)} %owner_ref.3) | copy-start | bytes 196
  66.8 0.6 copy-start.6
  67.4 11.2 %all-to-all-start.2 = ((bf16[16,16,128]{2,1,0:T(8,128)(2,1)}), bf16[16,16,128]{2,1,0:T(8,128)(2,1)S(1)}, u32[]{:S(2)}, u32[]{:S(2)}) async-start(bf16[16,16,128]{2,1,0:T(8,128)(2,1)} %copy-done.6), calls=%async_computation.2 | async-start | bytes 131072 | tf_op jit(solution)/shard_map/all_to_all | solution.py:196

commit v3 on v1

--- a/solution.py
+++ b/solution.py
@@ -68,36 +68,31 @@
     lax.fori_loop(0, homes, home, 0)
 
 
-def owner_kernel(slab_ref, weights_ref, ham_hbm, margin_hbm, out_ref, ham_ref, margin_ref, density_ref, sems):
+def change_kernel(ham_ref, margin_ref, out_ref):
+    homes, rows, width = out_ref.shape
+    for c in range(homes):
+        out_ref[c, :, : width // 2] = ham_ref[2 * c : 2 * c + 2].reshape(rows, width // 2)
+        out_ref[c, :, width // 2 :] = margin_ref[2 * c : 2 * c + 2].reshape(rows, width // 2)
+
+
+def owner_kernel(slab_ref, weights_ref, change_ref, out_ref, density_ref):
     chunks, homes, states, width = slab_ref.shape
     half = width // 2
-    copy_ham = pltpu.make_async_copy(ham_hbm, ham_ref, sems.at[0])
-    copy_margin = pltpu.make_async_copy(margin_hbm, margin_ref, sems.at[1])
-    copy_ham.start()
-    copy_margin.start()
-    for c in range(homes):
-        pair = slab_ref[:, c].reshape(chunks * states, width)
-        density_ref[c] = jnp.dot(weights_ref[...], pair, preferred_element_type=F32).astype(BF16)
-    copy_ham.wait()
-    copy_margin.wait()
+    slabs = jnp.concatenate([slab_ref[:, c].reshape(chunks * states, width) for c in range(homes)], axis=1)
+    density_ref[...] = jnp.dot(weights_ref[...], slabs, preferred_element_type=F32).astype(BF16)
     row = lax.broadcasted_iota(jnp.int32, (half, width), 0)
     lane = lax.broadcasted_iota(jnp.int32, (half, width), 1)
     masks = [lane == row + half * k for k in range(2)]
+    slim = lax.broadcasted_iota(jnp.int32, (8, width), 0)
     for c in range(homes):
-        change = jnp.concatenate(
-            [ham_ref[2 * c : 2 * c + 2].reshape(6 * half, width), margin_ref[2 * c : 2 * c + 2].reshape(6 * half, width)],
-            axis=1,
-        )
-        product = jnp.dot(change, density_ref[c], preferred_element_type=F32)
+        product = jnp.dot(change_ref[c], density_ref[:, c * width : (c + 1) * width], preferred_element_type=F32)
         product = product.reshape(2, 3, half, width)
-        parts = []
+        force = jnp.zeros((8, width), F32)
         for x in range(3):
             kept = jnp.where(masks[0], product[0, x], 0.0) + jnp.where(masks[1], product[1, x], 0.0)
-            parts.append(jnp.sum(kept, axis=0, keepdims=True))
-        force = jnp.concatenate(parts + [jnp.zeros((5, width), F32)], axis=0)
-        high = force.astype(BF16)
-        low = (force - high.astype(F32)).astype(BF16)
-        out_ref[c] = jnp.concatenate([high.astype(F32), low.astype(F32)], axis=0).astype(BF16)
+            force = jnp.where(slim == x, jnp.sum(kept, axis=0, keepdims=True), force)
+        high = force.astype(BF16).astype(F32)
+        out_ref[c] = jnp.concatenate([high, force - high], axis=0).astype(BF16)
 
 
 def hot_kernel(owner_ref, atom_ref, out_ref, rows_ref):
@@ -186,6 +181,10 @@
         [(panel_t * occ[None, :]).astype(BF16), (panel_t * -eweight[None, :]).astype(BF16)], axis=0
     )
 
+    weights, ham, margin, owner = lax.optimization_barrier(
+        (weights, hamiltonian_change, margin_change, tile_owner)
+    )
+
     device = row_index * columns + col_index
     atom = lax.dynamic_slice_in_dim(basis_atom, device * blocks * block_rows, blocks * block_rows)
     atom = (atom - device * ATOMS_DEV).reshape(blocks, block_rows)
@@ -198,21 +197,26 @@
         out_shape=jax.ShapeDtypeStruct((columns, width, atoms_padded), BF16),
         scratch_shapes=[pltpu.VMEM((columns, width), jnp.int32)],
         cost_estimate=pl.CostEstimate(flops=4 << 20, bytes_accessed=1 << 20, transcendentals=0),
-    )(tile_owner, atom)
-
+        compiler_params=pltpu.CompilerParams(vmem_limit_bytes=8 << 20),
+    )(owner, atom)
+
+    change = pl.pallas_call(
+        change_kernel,
+        in_specs=[whole(), whole()],
+        out_specs=whole(),
+        out_shape=jax.ShapeDtypeStruct((columns, 6 * block_rows, 2 * width), BF16),
+        cost_estimate=pl.CostEstimate(flops=1 << 20, bytes_accessed=6 << 20, transcendentals=0),
+        compiler_params=pltpu.CompilerParams(vmem_limit_bytes=16 << 20),
+    )(ham, margin)
+    slabs, weights, change, hot = lax.optimization_barrier((slabs, weights, change, hot))
     force = pl.pallas_call(
         owner_kernel,
-        in_specs=[whole(), whole(), whole(pl.ANY), whole(pl.ANY)],
+        in_specs=[whole(), whole(), whole()],
         out_specs=whole(),
         out_shape=jax.ShapeDtypeStruct((columns, 16, width), BF16),
-        scratch_shapes=[
-            pltpu.VMEM(hamiltonian_change.shape, BF16),
-            pltpu.VMEM(margin_change.shape, BF16),
-            pltpu.VMEM((columns, 2 * width, width), BF16),
-            pltpu.SemaphoreType.DMA((2,)),
-        ],
-        compiler_params=pltpu.CompilerParams(vmem_limit_bytes=32 << 20),
-    )(slabs, weights, hamiltonian_change, margin_change)
+        scratch_shapes=[pltpu.VMEM((2 * width, columns * width), BF16)],
+        compiler_params=pltpu.CompilerParams(vmem_limit_bytes=16 << 20),
+    )(slabs, weights, change)
 
     returned = swap(force)
     return pl.pallas_call(
@@ -220,6 +224,7 @@
         in_specs=[whole(), whole()],
         out_specs=whole(),
         out_shape=jax.ShapeDtypeStruct((3, ATOMS_DEV), F32),
+        compiler_params=pltpu.CompilerParams(vmem_limit_bytes=8 << 20),
     )(returned, hot)
 
 

time: 74.1 us -> 70 us (0.945)
  blocking collectives: 0 us -> 11.1 us
  waiting for transfers between devices: 34.4 us -> 24.1 us
  starting transfers between devices: 20.1 us -> 17.1 us
  Pallas kernels: 12.3 us -> 10.6 us
    all_to_all x0 -> x1, blocking collectives: none -> 11.1 us  [swap(): return lax.all_to_all(x, 'col', split_axis=0, concat_axis=0, tiled=True)]
    all_to_all x3 -> x2, waiting for transfers between devices: 28.8 us -> 18.5 us  [swap(): return lax.all_to_all(x, 'col', split_axis=0, concat_axis=0, tiled=True)]
    all_to_all x3 -> x2, starting transfers between devices: 15.7 us -> 12.7 us  [swap(): return lax.all_to_all(x, 'col', split_axis=0, concat_axis=0, tiled=True)]
    pallas_call x1, Pallas kernels: 2.11 us -> 0.85 us  [per_device(): pl.pallas_call(gather_kernel, in_specs=[whole(), whole()], out_specs=whol...]
    pallas_call x1, Pallas kernels: 2.3 us -> 1.16 us  [per_device(): pl.pallas_call(hot_kernel, in_specs=[whole(SMEM), whole()], out_specs=who...]
    pallas_call x1 -> x2, Pallas kernels: 3.09 us -> 3.77 us  [the longest x1 3.23 us: per_device(): pl.pallas_call(owner_kernel, in_specs=[whole(), whole(), whole()], out_sp...]
    unnamed x14 -> x18, local copies, waits for them, and re-layouts: 4.77 us -> 5.24 us
  transfers between devices with their start and end apart: 6 -> 5, of which waited for: 6 -> 5; matrix products, arithmetic and copies ran while one was open for 2% -> 2% of each run, Pallas kernels for 5% -> 5%
where the time goes in v3:
time: 70 us; the launch traced here: 69.6 us
  waiting for transfers between devices  24.1 us (34%)
  starting transfers between devices  17.1 us (24%)
  blocking collectives  11.1 us (16%)
  Pallas kernels  10.6 us (15%)
  local copies, waits for them, and re-layouts  5.44 us (8%)
  other arithmetic  0.98 us (1%)
    all_to_all x2, waiting for transfers between devices, swap(): return lax.all_to_all(x, 'col', split_axis=0, concat_axis=0, tiled=True)  18.5 us
    all_to_all x2, starting transfers between devices, swap(): return lax.all_to_all(x, 'col', split_axis=0, concat_axis=0, tiled=True)  12.7 us
    all_to_all x1, blocking collectives, swap(): return lax.all_to_all(x, 'col', split_axis=0, concat_axis=0, tiled=True)  11.1 us
    ppermute x3, waiting for transfers between devices, per_device(): lax.ppermute(panel, 'row', [(i, i + reach) for i in range(reach)])  5.56 us
    unnamed x18, local copies, waits for them, and re-layouts  5.24 us
    ppermute x3, starting transfers between devices, per_device(): lax.ppermute(panel, 'row', [(i, i + reach) for i in range(reach)])  4.43 us
    pallas_call x1, Pallas kernels, per_device(): pl.pallas_call(owner_kernel, in_specs=[whole(), whole(), whole()], out_sp...  3.23 us
    pallas_call x1, Pallas kernels, per_device(): pl.pallas_call(pack_kernel, in_specs=[whole(SMEM), whole()], out_specs=wh...  1.86 us
  transfers between devices with their start and end apart: 5, of which 5 were waited for; matrix products, arithmetic and copies ran while one was open for 2% of the time, Pallas kernels for 5%

profile of v3, /device:TPU:0, one launch (start us, length us, event | category | flops | bytes accessed | tf_op | source)
XLA Modules:
  0.0 69.6 jit_solution(9919497680675045823)
XLA Ops:
  0.0 1.5 %shard_map.73 = bf16[16,48,128]{2,1,0:T(8,128)(2,1)} custom-call(s32[16]{0:T(128)} %owner_ref.2, bf16[32,16384]{1,0:T(8,128)(2,1)} %slab_ref.1), custom_call_target="tpu_custom_call" | custom-call | tf_op jit(solution)/shard_map/pallas_call | solution.py:144
  1.5 8.1 %all-to-all-start = ((bf16[16,48,128]{2,1,0:T(8,128)(2,1)}), bf16[16,48,128]{2,1,0:T(8,128)(2,1)S(1)}, u32[]{:S(2)}, u32[]{:S(2)}) async-start(bf16[16,48,128]{2,1,0:T(8,128)(2,1)} %shard_map.73), calls=%async_computation | async-start | bytes 393216 | tf_op jit(solution)/shard_map/all_to_all | solution.py:142
  9.7 1.5 %shard_map.74.doubled_ref = bf16[16,17,32,128]{3,2,1,0:T(8,128)(2,1)S(1)} custom-call(bf16[32,16384]{1,0:T(8,128)(2,1)S(1)} %copy-done.1), custom_call_target="tpu_custom_call" | custom-call | flops 4194304 | bytes 3145728 | tf_op jit(solution)/shard_map/pallas_call | solution.py:152
  11.1 6.7 %all-to-all-done = bf16[16,48,128]{2,1,0:T(8,128)(2,1)S(1)} async-done(((bf16[16,48,128]{2,1,0:T(8,128)(2,1)}), bf16[16,48,128]{2,1,0:T(8,128)(2,1)S(1)}, u32[]{:S(2)}, u32[]{:S(2)}) %all-to-all-start) | async-done | bytes 196640 | tf_op jit(solution)/shard_map/all_to_all | solution.py:142
  17.8 1.9 %shard_map.75 = bf16[16,16,32,128]{3,2,1,0:T(8,128)(2,1)S(1)} custom-call(s32[16,32]{1,0:T(8,128)S(1)} %fusion.2.table_ref, bf16[16,17,32,128]{3,2,1,0:T(8,128)(2,1)S(1)} %shard_map.74.doubled_ref), custom_call_target="tpu_custom_call" | custom-call | tf_op jit(solution)/shard_map/pallas_call | solution.py:162
  19.7 1.3 %copy-done = bf16[16,16,32,128]{3,2,1,0:T(8,128)(2,1)} copy-done((bf16[16,16,32,128]{3,2,1,0:T(8,128)(2,1)}, bf16[16,16,32,128]{3,2,1,0:T(8,128)(2,1)S(1)}, u32[]{:S(2)}) %copy-start) | copy-done | bytes 2097176
  21.0 4.6 %all-to-all-start.1 = ((bf16[16,16,32,128]{3,2,1,0:T(8,128)(2,1)}), bf16[16,16,32,128]{3,2,1,0:T(8,128)(2,1)}, u32[]{:S(2)}, u32[]{:S(2)}) async-start(bf16[16,16,32,128]{3,2,1,0:T(8,128)(2,1)} %copy-done), calls=%async_computation.1 | async-start | bytes 4194304 | tf_op jit(solution)/shard_map/all_to_all | solution.py:142
  25.7 1.3 %collective-permute-start = (bf16[16,32,128]{2,1,0:T(8,128)(2,1)S(1)}, bf16[16,32,128]{2,1,0:T(8,128)(2,1)S(1)}, u32[]{:S(2)}, u32[]{:S(2)}) collective-permute-start(bf16[16,32,128]{2,1,0:T(8,128)(2,1)S(1)} %slice_select_fusion), channel_id=1, source_target_pairs={{0,16},{1,17},{2,18},{3,19},{4,20},{5,21},{6,22},{7,23},{8,24},{9,... | collective-permute-start | bytes 393224 | tf_op jit(solution)/shard_map/ppermute | solution.py:175
  27.0 1.0 %collective-permute-done = bf16[16,32,128]{2,1,0:T(8,128)(2,1)S(1)} collective-permute-done((bf16[16,32,128]{2,1,0:T(8,128)(2,1)S(1)}, bf16[16,32,128]{2,1,0:T(8,128)(2,1)S(1)}, u32[]{:S(2)}, u32[]{:S(2)}) %collective-permute-start) | collective-permute-done | bytes 131104 | tf_op jit(solution)/shard_map/ppermute | solution.py:175
  27.9 1.8 %collective-permute-start.1 = (bf16[16,32,128]{2,1,0:T(8,128)(2,1)S(1)}, bf16[16,32,128]{2,1,0:T(8,128)(2,1)S(1)}, u32[]{:S(2)}, u32[]{:S(2)}) collective-permute-start(bf16[16,32,128]{2,1,0:T(8,128)(2,1)S(1)} %fusion.3), channel_id=1, source_target_pairs={{0,32},{16,48},{1,33},{17,49},{2,34},{18,50},{3,35},{19,51},{4,36}... | collective-permute-start | bytes 393224 | tf_op jit(solution)/shard_map/ppermute | solution.py:175
  29.8 3.0 %collective-permute-done.1 = bf16[16,32,128]{2,1,0:T(8,128)(2,1)S(1)} collective-permute-done((bf16[16,32,128]{2,1,0:T(8,128)(2,1)S(1)}, bf16[16,32,128]{2,1,0:T(8,128)(2,1)S(1)}, u32[]{:S(2)}, u32[]{:S(2)}) %collective-permute-start.1) | collective-permute-done | bytes 131104 | tf_op jit(solution)/shard_map/ppermute | solution.py:175
  32.8 1.3 %collective-permute-start.2 = (bf16[16,32,128]{2,1,0:T(8,128)(2,1)S(1)}, bf16[16,32,128]{2,1,0:T(8,128)(2,1)S(1)}, u32[]{:S(2)}, u32[]{:S(2)}) collective-permute-start(bf16[16,32,128]{2,1,0:T(8,128)(2,1)S(1)} %add.16), channel_id=1, source_target_pairs={{0,64},{16,80},{32,96},{48,112},{1,65},{17,81},{33,97},{49,113},{2... | collective-permute-start | bytes 393224 | tf_op jit(solution)/shard_map/ppermute | solution.py:175
  34.1 0.7 %dynamic-slice_subtract_fusion = s32[1024]{0:T(1024)S(1)} fusion(s32[131072]{0:T(1024)} %param.13, s32[]{:T(128)S(6)} %select_n.13, s32[]{:T(128)S(6)} %mul.38), kind=kLoop, calls=%fused_computation.10 | loop fusion | flops 1024 | bytes 8200 | tf_op jit(solution)/shard_map/sub | solution.py:190
  35.0 1.6 %collective-permute-done.2 = bf16[16,32,128]{2,1,0:T(8,128)(2,1)S(1)} collective-permute-done((bf16[16,32,128]{2,1,0:T(8,128)(2,1)S(1)}, bf16[16,32,128]{2,1,0:T(8,128)(2,1)S(1)}, u32[]{:S(2)}, u32[]{:S(2)}) %collective-permute-start.2) | collective-permute-done | bytes 131104 | tf_op jit(solution)/shard_map/ppermute | solution.py:175
  36.7 0.1 copy.15
  36.9 1.4 %copy-done.4 = bf16[32,3,64,128]{3,2,1,0:T(8,128)(2,1)S(1)} copy-done((bf16[32,3,64,128]{3,2,1,0:T(8,128)(2,1)S(1)}, bf16[32,3,64,128]{3,2,1,0:T(8,128)(2,1)}, u32[]{:S(2)}) %copy-start.4) | copy-done | bytes 1572888
  38.3 1.4 %copy-done.5 = bf16[32,3,64,128]{3,2,1,0:T(8,128)(2,1)S(1)} copy-done((bf16[32,3,64,128]{3,2,1,0:T(8,128)(2,1)S(1)}, bf16[32,3,64,128]{3,2,1,0:T(8,128)(2,1)}, u32[]{:S(2)}) %copy-start.5) | copy-done | bytes 1572888
  39.7 0.5 shard_map.76.change_ref
  40.4 1.2 %shard_map.77.hot_ref = bf16[16,128,256]{2,1,0:T(8,128)(2,1)S(1)} custom-call(s32[16]{0:T(128)S(1)} %copy-done.6, s32[16,128]{1,0:T(8,128)S(1)} %pad_add_fusion.atom_ref), custom_call_target="tpu_custom_call" | custom-call | flops 4194304 | bytes 1048576 | tf_op jit(solution)/shard_map/pallas_call | solution.py:193
  41.6 1.0 %copy-done.2 = bf16[16,128,256]{2,1,0:T(8,128)(2,1)} copy-done((bf16[16,128,256]{2,1,0:T(8,128)(2,1)}, bf16[16,128,256]{2,1,0:T(8,128)(2,1)S(1)}, u32[]{:S(2)}) %copy-start.2) | copy-done | bytes 1048600
  42.5 11.8 %all-to-all-done.1.slab_ref = bf16[16,16,32,128]{3,2,1,0:T(8,128)(2,1)} async-done(((bf16[16,16,32,128]{3,2,1,0:T(8,128)(2,1)}), bf16[16,16,32,128]{3,2,1,0:T(8,128)(2,1)}, u32[]{:S(2)}, u32[]{:S(2)}) %all-to-all-start.1) | async-done | bytes 2097184 | tf_op jit(solution)/shard_map/all_to_all | solution.py:142
  54.4 3.2 %shard_map.78 = bf16[16,16,128]{2,1,0:T(8,128)(2,1)S(1)} custom-call(bf16[16,16,32,128]{3,2,1,0:T(8,128)(2,1)} %all-to-all-done.1.slab_ref, bf16[256,512]{1,0:T(8,128)(2,1)S(1)} %pad_maximum_fusion.weights_ref, bf16[16,384,256]{2,1,0:T(8,128)(2,1)S(1)} %shard_map.76.change_ref), custom_call_target="tpu_custom_call" | custom-call | tf_op jit(solution)/shard_map/pallas_call | solution.py:212
  57.6 11.1 %all_to_all.15.force_ref = bf16[16,16,128]{2,1,0:T(8,128)(2,1)S(1)} all-to-all(bf16[16,16,128]{2,1,0:T(8,128)(2,1)S(1)} %shard_map.78), channel_id=1, replica_groups=mesh['row'=8,'col'=16] {'col'}, dimensions={0} | all-to-all | bytes 131072 | tf_op jit(solution)/shard_map/all_to_all | solution.py:142
  68.7 0.8 %shard_map.79 = f32[3,160]{1,0:T(4,128)} custom-call(bf16[16,16,128]{2,1,0:T(8,128)(2,1)S(1)} %all_to_all.15.force_ref, bf16[16,128,256]{2,1,0:T(8,128)(2,1)S(1)} %copy-done.3), custom_call_target="tpu_custom_call" | custom-call | tf_op jit(solution)/shard_map/pallas_call | solution.py:222
  (27 shorter events, 0.5 us)
Async XLA Ops:
  0.0 9.6 %copy-start.1 = (bf16[32,16384]{1,0:T(8,128)(2,1)S(1)}, bf16[32,16384]{1,0:T(8,128)(2,1)}, u32[]{:S(2)}) copy-start(bf16[32,16384]{1,0:T(8,128)(2,1)} %slab_ref.1) | copy-start | bytes 3145732
  1.5 16.3 %all-to-all-start = ((bf16[16,48,128]{2,1,0:T(8,128)(2,1)}), bf16[16,48,128]{2,1,0:T(8,128)(2,1)S(1)}, u32[]{:S(2)}, u32[]{:S(2)}) async-start(bf16[16,48,128]{2,1,0:T(8,128)(2,1)} %shard_map.73), calls=%async_computation | async-start | bytes 393216 | tf_op jit(solution)/shard_map/all_to_all | solution.py:142
  19.7 1.3 %copy-start = (bf16[16,16,32,128]{3,2,1,0:T(8,128)(2,1)}, bf16[16,16,32,128]{3,2,1,0:T(8,128)(2,1)S(1)}, u32[]{:S(2)}) copy-start(bf16[16,16,32,128]{3,2,1,0:T(8,128)(2,1)S(1)} %shard_map.75) | copy-start | bytes 6291460
  21.0 8.8 %copy-start.7 = (s32[512]{0:T(512)S(1)}, s32[512]{0:T(512)}, u32[]{:S(2)}) copy-start(s32[512]{0:T(512)} %param.8) | copy-start | bytes 6148
  21.0 8.8 %copy-start.8 = (f32[512]{0:T(512)S(1)}, f32[512]{0:T(512)}, u32[]{:S(2)}) copy-start(f32[512]{0:T(512)} %param.9) | copy-start | bytes 6148
  21.0 33.3 %all-to-all-start.1 = ((bf16[16,16,32,128]{3,2,1,0:T(8,128)(2,1)}), bf16[16,16,32,128]{3,2,1,0:T(8,128)(2,1)}, u32[]{:S(2)}, u32[]{:S(2)}) async-start(bf16[16,16,32,128]{3,2,1,0:T(8,128)(2,1)} %copy-done), calls=%async_computation.1 | async-start | bytes 4194304 | tf_op jit(solution)/shard_map/all_to_all | solution.py:142
  25.7 2.3 %collective-permute-start = (bf16[16,32,128]{2,1,0:T(8,128)(2,1)S(1)}, bf16[16,32,128]{2,1,0:T(8,128)(2,1)S(1)}, u32[]{:S(2)}, u32[]{:S(2)}) collective-permute-start(bf16[16,32,128]{2,1,0:T(8,128)(2,1)S(1)} %slice_select_fusion), channel_id=1, source_target_pairs={{0,16},{1,17},{2,18},{3,19},{4,20},{5,21},{6,22},{7,23},{8,24},{9,... | collective-permute-start | bytes 393224 | tf_op jit(solution)/shard_map/ppermute | solution.py:175
  27.9 4.8 %collective-permute-start.1 = (bf16[16,32,128]{2,1,0:T(8,128)(2,1)S(1)}, bf16[16,32,128]{2,1,0:T(8,128)(2,1)S(1)}, u32[]{:S(2)}, u32[]{:S(2)}) collective-permute-start(bf16[16,32,128]{2,1,0:T(8,128)(2,1)S(1)} %fusion.3), channel_id=1, source_target_pairs={{0,32},{16,48},{1,33},{17,49},{2,34},{18,50},{3,35},{19,51},{4,36}... | collective-permute-start | bytes 393224 | tf_op jit(solution)/shard_map/ppermute | solution.py:175
  32.8 3.8 %collective-permute-start.2 = (bf16[16,32,128]{2,1,0:T(8,128)(2,1)S(1)}, bf16[16,32,128]{2,1,0:T(8,128)(2,1)S(1)}, u32[]{:S(2)}, u32[]{:S(2)}) collective-permute-start(bf16[16,32,128]{2,1,0:T(8,128)(2,1)S(1)} %add.16), channel_id=1, source_target_pairs={{0,64},{16,80},{32,96},{48,112},{1,65},{17,81},{33,97},{49,113},{2... | collective-permute-start | bytes 393224 | tf_op jit(solution)/shard_map/ppermute | solution.py:175
  36.9 1.4 %copy-start.4 = (bf16[32,3,64,128]{3,2,1,0:T(8,128)(2,1)S(1)}, bf16[32,3,64,128]{3,2,1,0:T(8,128)(2,1)}, u32[]{:S(2)}) copy-start(bf16[32,3,64,128]{3,2,1,0:T(8,128)(2,1)} %ham_ref) | copy-start | bytes 4718596
  38.3 1.4 %copy-start.5 = (bf16[32,3,64,128]{3,2,1,0:T(8,128)(2,1)S(1)}, bf16[32,3,64,128]{3,2,1,0:T(8,128)(2,1)}, u32[]{:S(2)}) copy-start(bf16[32,3,64,128]{3,2,1,0:T(8,128)(2,1)} %margin_ref) | copy-start | bytes 4718596
  39.7 0.7 copy-start.6
  41.5 1.0 %copy-start.2 = (bf16[16,128,256]{2,1,0:T(8,128)(2,1)}, bf16[16,128,256]{2,1,0:T(8,128)(2,1)S(1)}, u32[]{:S(2)}) copy-start(bf16[16,128,256]{2,1,0:T(8,128)(2,1)S(1)} %shard_map.77.hot_ref) | copy-start | bytes 3145732
  54.3 14.4 %copy-start.3 = (bf16[16,128,256]{2,1,0:T(8,128)(2,1)S(1)}, bf16[16,128,256]{2,1,0:T(8,128)(2,1)}, u32[]{:S(2)}) copy-start(bf16[16,128,256]{2,1,0:T(8,128)(2,1)} %copy-done.2) | copy-start | bytes 3145732

commit v4 on v3

--- a/solution.py
+++ b/solution.py
@@ -6,6 +6,12 @@
 from jax.sharding import PartitionSpec as P
 
 ATOMS_DEV = 160
+ORDER = (0, 1, 2, 3, 4, 5, 6, 7, 8, 9, 10, 11, 12, 13, 14, 15)
+FIRST = (7, 8, 6, 14, 1, 3, 9, 12, 13, 0, 4, 11, 5, 10, 2, 15)
+HEARD = tuple(FIRST.index(column) for column in range(len(FIRST)))
+BACK = (2, 8, 6, 14, 9, 3, 1, 5, 7, 15, 4, 11, 12, 13, 10, 0)
+RETURN = tuple(BACK.index(column) for column in range(len(BACK)))
+PLACE = tuple(ORDER.index(column) for column in range(len(ORDER)))
 BF16 = jnp.bfloat16
 F32 = jnp.float32
 VMEM = pltpu.VMEM
@@ -40,32 +46,36 @@
     columns, blocks, states, width = out_ref.shape
     blocks -= 1
     low = lax.broadcasted_iota(jnp.int32, (states, width), 1) < width // 2
-
-    def home(c, carry):
+    for place in range(columns):
         for j in range(blocks // 2):
-            start = pl.multiple_of((c * (blocks // 2) + j) * width, width)
-            tile = slab_ref[:, pl.ds(start, width)].astype(F32)
+            start = (FIRST[place] * (blocks // 2) + j) * width
+            tile = slab_ref[:, start : start + width].astype(F32)
             turned = pltpu.roll(tile, width // 2, 1)
-            out_ref[c, 2 * j] = jnp.where(low, tile, turned).astype(BF16)
-            out_ref[c, 2 * j + 1] = jnp.where(low, turned, tile).astype(BF16)
-        out_ref[c, blocks] = jnp.zeros((states, width), BF16)
-        return carry
-
-    lax.fori_loop(0, columns, home, 0)
+            out_ref[place, 2 * j] = jnp.where(low, tile, turned).astype(BF16)
+            out_ref[place, 2 * j + 1] = jnp.where(low, turned, tile).astype(BF16)
+        out_ref[place, blocks] = jnp.zeros((states, width), BF16)
 
 
 def pack_kernel(table_ref, doubled_ref, out_ref):
     columns, homes, states, width = out_ref.shape
     low = lax.broadcasted_iota(jnp.int32, (states, width), 1) < width // 2
 
-    def home(c, carry):
+    def home(h, carry):
         for o in range(columns):
-            left = doubled_ref[c, table_ref[c, 2 * o]]
-            right = doubled_ref[c, table_ref[c, 2 * o + 1]]
-            out_ref[o, c] = jnp.where(low, left, right)
+            left = doubled_ref[h, table_ref[h, 2 * o]]
+            right = doubled_ref[h, table_ref[h, 2 * o + 1]]
+            out_ref[PLACE[o], h] = jnp.where(low, left, right)
         return carry
 
     lax.fori_loop(0, homes, home, 0)
+
+
+def weights_kernel(panel_ref, scale_ref, out_ref):
+    columns, states, width = panel_ref.shape
+    panel = jnp.concatenate([panel_ref[HEARD[column]] for column in ORDER], axis=0).astype(F32).T
+    scale = jnp.concatenate([scale_ref[:, column * states : (column + 1) * states] for column in ORDER], axis=1)
+    out_ref[:width, :] = (panel * scale[0:1, :]).astype(BF16)
+    out_ref[width:, :] = (panel * scale[1:2, :]).astype(BF16)
 
 
 def change_kernel(ham_ref, margin_ref, out_ref):
@@ -75,24 +85,41 @@
         out_ref[c, :, width // 2 :] = margin_ref[2 * c : 2 * c + 2].reshape(rows, width // 2)
 
 
-def owner_kernel(slab_ref, weights_ref, change_ref, out_ref, density_ref):
+def owner_kernel(slab_any, weights_ref, change_ref, out_ref, slab_ref, total_ref, density_ref, sems):
     chunks, homes, states, width = slab_ref.shape
     half = width // 2
-    slabs = jnp.concatenate([slab_ref[:, c].reshape(chunks * states, width) for c in range(homes)], axis=1)
-    density_ref[...] = jnp.dot(weights_ref[...], slabs, preferred_element_type=F32).astype(BF16)
+    share = chunks // 2
+    copies = []
+    for p in range(2):
+        here = pl.ds(p * share, share)
+        copies.append(pltpu.make_async_copy(slab_any.at[here], slab_ref.at[here], sems.at[p]))
+        copies[p].start()
+    for p in range(2):
+        copies[p].wait()
+        slabs = jnp.concatenate(
+            [slab_ref[p * share : (p + 1) * share, c].reshape(share * states, width) for c in range(homes)], axis=1
+        )
+        part = jnp.dot(
+            weights_ref[:, p * share * states : (p + 1) * share * states], slabs, preferred_element_type=F32
+        )
+        if p == 0:
+            total_ref[...] = part
+        else:
+            density_ref[...] = (total_ref[...] + part).astype(BF16)
     row = lax.broadcasted_iota(jnp.int32, (half, width), 0)
     lane = lax.broadcasted_iota(jnp.int32, (half, width), 1)
     masks = [lane == row + half * k for k in range(2)]
     slim = lax.broadcasted_iota(jnp.int32, (8, width), 0)
-    for c in range(homes):
-        product = jnp.dot(change_ref[c], density_ref[:, c * width : (c + 1) * width], preferred_element_type=F32)
+    for h in range(homes):
+        c = FIRST[h]
+        product = jnp.dot(change_ref[c], density_ref[:, h * width : (h + 1) * width], preferred_element_type=F32)
         product = product.reshape(2, 3, half, width)
         force = jnp.zeros((8, width), F32)
         for x in range(3):
             kept = jnp.where(masks[0], product[0, x], 0.0) + jnp.where(masks[1], product[1, x], 0.0)
             force = jnp.where(slim == x, jnp.sum(kept, axis=0, keepdims=True), force)
         high = force.astype(BF16).astype(F32)
-        out_ref[c] = jnp.concatenate([high, force - high], axis=0).astype(BF16)
+        out_ref[RETURN[c]] = jnp.concatenate([high, force - high], axis=0).astype(BF16)
 
 
 def hot_kernel(owner_ref, atom_ref, out_ref, rows_ref):
@@ -122,7 +149,7 @@
     columns = force_ref.shape[0]
     total = jnp.zeros((force_ref.shape[1], hot_ref.shape[2]), F32)
     for o in range(columns):
-        total = total + jnp.dot(force_ref[o], hot_ref[o], preferred_element_type=F32)
+        total = total + jnp.dot(force_ref[RETURN[o]], hot_ref[o], preferred_element_type=F32)
     out_ref[...] = 2.0 * (total[0:3, : out_ref.shape[1]] + total[8:11, : out_ref.shape[1]])
 
 
@@ -138,8 +165,8 @@
     block_rows = margin_change.shape[2]
     width = margin_change.shape[3]
 
-    def swap(x):
-        return lax.all_to_all(x, "col", split_axis=0, concat_axis=0, tiled=True)
+    def swap(x, groups=None):
+        return lax.all_to_all(x, "col", split_axis=0, concat_axis=0, tiled=True, axis_index_groups=groups)
 
     announced = pl.pallas_call(
         announce_kernel,
@@ -148,7 +175,7 @@
         out_specs=pl.BlockSpec((columns, states + 16, width), lambda i: (0, 0, 0)),
         out_shape=jax.ShapeDtypeStruct((columns, states + 16, width), BF16),
     )(tile_owner, eigvec_slab)
-    heard = swap(announced)
+    heard = swap(announced, [list(FIRST)])
     doubled = pl.pallas_call(
         double_kernel,
         in_specs=[whole()],
@@ -166,7 +193,7 @@
         out_shape=jax.ShapeDtypeStruct((columns, columns, states, width), BF16),
         compiler_params=pltpu.CompilerParams(vmem_limit_bytes=16 << 20),
     )(table, doubled)
-    slabs = swap(packed)
+    slabs = swap(packed, [list(ORDER)])
 
     panel = heard[:, :states, :]
     panel = jnp.where(row_index == 0, panel, jnp.zeros_like(panel))
@@ -176,10 +203,14 @@
         reach *= 2
     occ = occupations.astype(F32)
     eweight = occ * energies
-    panel_t = panel.reshape(columns * states, width).T.astype(F32)
-    weights = jnp.concatenate(
-        [(panel_t * occ[None, :]).astype(BF16), (panel_t * -eweight[None, :]).astype(BF16)], axis=0
-    )
+    weights = pl.pallas_call(
+        weights_kernel,
+        in_specs=[whole(), whole()],
+        out_specs=whole(),
+        out_shape=jax.ShapeDtypeStruct((2 * width, columns * states), BF16),
+        cost_estimate=pl.CostEstimate(flops=1 << 20, bytes_accessed=1 << 19, transcendentals=0),
+        compiler_params=pltpu.CompilerParams(vmem_limit_bytes=8 << 20),
+    )(panel, jnp.stack([occ, -eweight]))
 
     weights, ham, margin, owner = lax.optimization_barrier(
         (weights, hamiltonian_change, margin_change, tile_owner)
@@ -211,14 +242,19 @@
     slabs, weights, change, hot = lax.optimization_barrier((slabs, weights, change, hot))
     force = pl.pallas_call(
         owner_kernel,
-        in_specs=[whole(), whole(), whole()],
+        in_specs=[whole(pl.ANY), whole(), whole()],
         out_specs=whole(),
         out_shape=jax.ShapeDtypeStruct((columns, 16, width), BF16),
-        scratch_shapes=[pltpu.VMEM((2 * width, columns * width), BF16)],
+        scratch_shapes=[
+            pltpu.VMEM(slabs.shape, BF16),
+            pltpu.VMEM((2 * width, columns * width), F32),
+            pltpu.VMEM((2 * width, columns * width), BF16),
+            pltpu.SemaphoreType.DMA((2,)),
+        ],
         compiler_params=pltpu.CompilerParams(vmem_limit_bytes=16 << 20),
     )(slabs, weights, change)
 
-    returned = swap(force)
+    returned = swap(force, [list(BACK)])
     return pl.pallas_call(
         gather_kernel,
         in_specs=[whole(), whole()],

time: 70 us -> 66.5 us (0.950)
  waiting for transfers between devices: 24.1 us -> 22.4 us
  blocking collectives: 11.1 us -> 9.83 us
  Pallas kernels: 10.6 us -> 9.39 us
  starting transfers between devices: 17.1 us -> 18 us
    all_to_all x2, waiting for transfers between devices: 18.5 us -> 16.8 us  [swap(): lax.all_to_all(x, 'col', split_axis=0, concat_axis=0, tiled=True, axis_in...]
    all_to_all x1, blocking collectives: 11.1 us -> 9.83 us  [swap(): lax.all_to_all(x, 'col', split_axis=0, concat_axis=0, tiled=True, axis_in...]
    pallas_call x1, Pallas kernels: 1.45 us -> 0.43 us  [per_device(): pl.pallas_call(double_kernel, in_specs=[whole()], out_specs=whole(), out_...]
    all_to_all x2, starting transfers between devices: 12.7 us -> 13.6 us  [swap(): lax.all_to_all(x, 'col', split_axis=0, concat_axis=0, tiled=True, axis_in...]
    pallas_call x1 -> x2, Pallas kernels: 3.23 us -> 3.05 us  [the longest x1 2.95 us: per_device(): pl.pallas_call(owner_kernel, in_specs=[whole(pl.ANY), whole(), whole()],...]
  transfers between devices with their start and end apart: 5 -> 5, of which waited for: 5 -> 5; matrix products, arithmetic and copies ran while one was open for 2% -> 1% of each run, Pallas kernels for 5% -> 3%
where the time goes in v4:
time: 66.5 us; the launch traced here: 66 us
  waiting for transfers between devices  22.4 us (34%)
  starting transfers between devices  18 us (27%)
  blocking collectives  9.83 us (15%)
  Pallas kernels  9.39 us (14%)
  local copies, waits for them, and re-layouts  5.28 us (8%)
  other arithmetic  0.91 us (1%)
    all_to_all x2, waiting for transfers between devices, swap(): lax.all_to_all(x, 'col', split_axis=0, concat_axis=0, tiled=True, axis_in...  16.8 us
    all_to_all x2, starting transfers between devices, swap(): lax.all_to_all(x, 'col', split_axis=0, concat_axis=0, tiled=True, axis_in...  13.6 us
    all_to_all x1, blocking collectives, swap(): lax.all_to_all(x, 'col', split_axis=0, concat_axis=0, tiled=True, axis_in...  9.83 us
    ppermute x3, waiting for transfers between devices, per_device(): lax.ppermute(panel, 'row', [(i, i + reach) for i in range(reach)])  5.55 us
    unnamed x18, local copies, waits for them, and re-layouts  5.21 us
    ppermute x3, starting transfers between devices, per_device(): lax.ppermute(panel, 'row', [(i, i + reach) for i in range(reach)])  4.42 us
    pallas_call x1, Pallas kernels, per_device(): pl.pallas_call(owner_kernel, in_specs=[whole(pl.ANY), whole(), whole()],...  2.95 us
    pallas_call x1, Pallas kernels, per_device(): pl.pallas_call(pack_kernel, in_specs=[whole(SMEM), whole()], out_specs=wh...  1.86 us
  transfers between devices with their start and end apart: 5, of which 5 were waited for; matrix products, arithmetic and copies ran while one was open for 1% of the time, Pallas kernels for 3%

profile of v4, /device:TPU:0, one launch (start us, length us, event | category | flops | bytes accessed | tf_op | source)
XLA Modules:
  0.0 66.0 jit_solution(4586171602448096574)
XLA Ops:
  0.0 1.5 %shard_map.73 = bf16[16,48,128]{2,1,0:T(8,128)(2,1)} custom-call(s32[16]{0:T(128)} %owner_ref.2, bf16[32,16384]{1,0:T(8,128)(2,1)} %slab_ref.1), custom_call_target="tpu_custom_call" | custom-call | tf_op jit(solution)/shard_map/pallas_call | solution.py:171
  1.5 8.7 %all-to-all-start = ((bf16[16,48,128]{2,1,0:T(8,128)(2,1)}), bf16[16,48,128]{2,1,0:T(8,128)(2,1)S(1)}, u32[]{:S(2)}, u32[]{:S(2)}) async-start(bf16[16,48,128]{2,1,0:T(8,128)(2,1)} %shard_map.73), calls=%async_computation | async-start | bytes 393216 | tf_op jit(solution)/shard_map/all_to_all | solution.py:169
  10.2 0.4 shard_map.74.doubled_ref
  10.7 5.2 %all-to-all-done = bf16[16,48,128]{2,1,0:T(8,128)(2,1)S(1)} async-done(((bf16[16,48,128]{2,1,0:T(8,128)(2,1)}), bf16[16,48,128]{2,1,0:T(8,128)(2,1)S(1)}, u32[]{:S(2)}, u32[]{:S(2)}) %all-to-all-start) | async-done | bytes 196640 | tf_op jit(solution)/shard_map/all_to_all | solution.py:169
  15.9 1.9 %shard_map.75 = bf16[16,16,32,128]{3,2,1,0:T(8,128)(2,1)S(1)} custom-call(s32[16,32]{1,0:T(8,128)S(1)} %bitcast.3, bf16[16,17,32,128]{3,2,1,0:T(8,128)(2,1)S(1)} %shard_map.74.doubled_ref), custom_call_target="tpu_custom_call" | custom-call | tf_op jit(solution)/shard_map/pallas_call | solution.py:189
  17.7 1.3 %copy-done = bf16[16,16,32,128]{3,2,1,0:T(8,128)(2,1)} copy-done((bf16[16,16,32,128]{3,2,1,0:T(8,128)(2,1)}, bf16[16,16,32,128]{3,2,1,0:T(8,128)(2,1)S(1)}, u32[]{:S(2)}) %copy-start) | copy-done | bytes 2097176
  19.1 4.9 %all-to-all-start.1 = ((bf16[16,16,32,128]{3,2,1,0:T(8,128)(2,1)}), bf16[16,16,32,128]{3,2,1,0:T(8,128)(2,1)}, u32[]{:S(2)}, u32[]{:S(2)}) async-start(bf16[16,16,32,128]{3,2,1,0:T(8,128)(2,1)} %copy-done), calls=%async_computation.1 | async-start | bytes 4194304 | tf_op jit(solution)/shard_map/all_to_all | solution.py:169
  24.0 1.3 %collective-permute-start = (bf16[16,32,128]{2,1,0:T(8,128)(2,1)S(1)}, bf16[16,32,128]{2,1,0:T(8,128)(2,1)S(1)}, u32[]{:S(2)}, u32[]{:S(2)}) collective-permute-start(bf16[16,32,128]{2,1,0:T(8,128)(2,1)S(1)} %slice_select_fusion), channel_id=1, source_target_pairs={{0,16},{1,17},{2,18},{3,19},{4,20},{5,21},{6,22},{7,23},{8,24},{9,... | collective-permute-start | bytes 393224 | tf_op jit(solution)/shard_map/ppermute | solution.py:202
  25.3 1.0 %collective-permute-done = bf16[16,32,128]{2,1,0:T(8,128)(2,1)S(1)} collective-permute-done((bf16[16,32,128]{2,1,0:T(8,128)(2,1)S(1)}, bf16[16,32,128]{2,1,0:T(8,128)(2,1)S(1)}, u32[]{:S(2)}, u32[]{:S(2)}) %collective-permute-start) | collective-permute-done | bytes 131104 | tf_op jit(solution)/shard_map/ppermute | solution.py:202
  26.3 1.8 %collective-permute-start.1 = (bf16[16,32,128]{2,1,0:T(8,128)(2,1)S(1)}, bf16[16,32,128]{2,1,0:T(8,128)(2,1)S(1)}, u32[]{:S(2)}, u32[]{:S(2)}) collective-permute-start(bf16[16,32,128]{2,1,0:T(8,128)(2,1)S(1)} %fusion), channel_id=1, source_target_pairs={{0,32},{16,48},{1,33},{17,49},{2,34},{18,50},{3,35},{19,51},{4,36}... | collective-permute-start | bytes 393224 | tf_op jit(solution)/shard_map/ppermute | solution.py:202
  28.2 2.9 %collective-permute-done.1 = bf16[16,32,128]{2,1,0:T(8,128)(2,1)S(1)} collective-permute-done((bf16[16,32,128]{2,1,0:T(8,128)(2,1)S(1)}, bf16[16,32,128]{2,1,0:T(8,128)(2,1)S(1)}, u32[]{:S(2)}, u32[]{:S(2)}) %collective-permute-start.1) | collective-permute-done | bytes 131104 | tf_op jit(solution)/shard_map/ppermute | solution.py:202
  31.1 1.3 %collective-permute-start.2 = (bf16[16,32,128]{2,1,0:T(8,128)(2,1)S(1)}, bf16[16,32,128]{2,1,0:T(8,128)(2,1)S(1)}, u32[]{:S(2)}, u32[]{:S(2)}) collective-permute-start(bf16[16,32,128]{2,1,0:T(8,128)(2,1)S(1)} %add.16), channel_id=1, source_target_pairs={{0,64},{16,80},{32,96},{48,112},{1,65},{17,81},{33,97},{49,113},{2... | collective-permute-start | bytes 393224 | tf_op jit(solution)/shard_map/ppermute | solution.py:202
  32.4 0.7 %dynamic-slice_subtract_fusion = s32[1024]{0:T(1024)S(1)} fusion(s32[131072]{0:T(1024)} %param.13, s32[]{:T(128)S(6)} %select_n.13, s32[]{:T(128)S(6)} %mul.16), kind=kLoop, calls=%fused_computation.4 | loop fusion | flops 1024 | bytes 8200 | tf_op jit(solution)/shard_map/sub | solution.py:221
  33.3 1.6 %collective-permute-done.2 = bf16[16,32,128]{2,1,0:T(8,128)(2,1)S(1)} collective-permute-done((bf16[16,32,128]{2,1,0:T(8,128)(2,1)S(1)}, bf16[16,32,128]{2,1,0:T(8,128)(2,1)S(1)}, u32[]{:S(2)}, u32[]{:S(2)}) %collective-permute-start.2) | collective-permute-done | bytes 131104 | tf_op jit(solution)/shard_map/ppermute | solution.py:202
  35.1 1.4 %copy-done.4 = bf16[32,3,64,128]{3,2,1,0:T(8,128)(2,1)S(1)} copy-done((bf16[32,3,64,128]{3,2,1,0:T(8,128)(2,1)S(1)}, bf16[32,3,64,128]{3,2,1,0:T(8,128)(2,1)}, u32[]{:S(2)}) %copy-start.4) | copy-done | bytes 1572888
  36.5 1.4 %copy-done.5 = bf16[32,3,64,128]{3,2,1,0:T(8,128)(2,1)S(1)} copy-done((bf16[32,3,64,128]{3,2,1,0:T(8,128)(2,1)S(1)}, bf16[32,3,64,128]{3,2,1,0:T(8,128)(2,1)}, u32[]{:S(2)}) %copy-start.5) | copy-done | bytes 1572888
  37.9 0.5 shard_map.77.change_ref
  38.5 0.1 copy-done.6
  38.6 1.2 %shard_map.78.hot_ref = bf16[16,128,256]{2,1,0:T(8,128)(2,1)S(1)} custom-call(s32[16]{0:T(128)S(1)} %copy-done.6, s32[16,128]{1,0:T(8,128)S(1)} %pad_add_fusion.atom_ref), custom_call_target="tpu_custom_call" | custom-call | flops 4194304 | bytes 1048576 | tf_op jit(solution)/shard_map/pallas_call | solution.py:224
  39.7 1.0 %copy-done.2 = bf16[16,128,256]{2,1,0:T(8,128)(2,1)} copy-done((bf16[16,128,256]{2,1,0:T(8,128)(2,1)}, bf16[16,128,256]{2,1,0:T(8,128)(2,1)S(1)}, u32[]{:S(2)}) %copy-start.2) | copy-done | bytes 1048600
  40.7 11.7 %all-to-all-done.1.slab_any = bf16[16,16,32,128]{3,2,1,0:T(8,128)(2,1)} async-done(((bf16[16,16,32,128]{3,2,1,0:T(8,128)(2,1)}), bf16[16,16,32,128]{3,2,1,0:T(8,128)(2,1)}, u32[]{:S(2)}, u32[]{:S(2)}) %all-to-all-start.1) | async-done | bytes 2097184 | tf_op jit(solution)/shard_map/all_to_all | solution.py:169
  52.4 2.9 %shard_map.79 = bf16[16,16,128]{2,1,0:T(8,128)(2,1)S(1)} custom-call(bf16[16,16,32,128]{3,2,1,0:T(8,128)(2,1)} %all-to-all-done.1.slab_any, bf16[256,512]{1,0:T(8,128)(2,1)S(1)} %shard_map.76.weights_ref, bf16[16,384,256]{2,1,0:T(8,128)(2,1)S(1)} %shard_map.77.change_ref), custom_call_target="tpu_custom_call" | custom-call | tf_op jit(solution)/shard_map/pallas_call | solution.py:243
  55.3 9.8 %all_to_all.15.force_ref = bf16[16,16,128]{2,1,0:T(8,128)(2,1)S(1)} all-to-all(bf16[16,16,128]{2,1,0:T(8,128)(2,1)S(1)} %shard_map.79), channel_id=1, replica_groups={{2,8,6,14,9,3,1,5,7,15,4,11,12,13,10,0},{18,24,22,30,25,19,17,21,23,31,..., dimensions={0} | all-to-all | bytes 131072 | tf_op jit(solution)/shard_map/all_to_all | solution.py:169
  65.1 0.8 %shard_map.80 = f32[3,160]{1,0:T(4,128)} custom-call(bf16[16,16,128]{2,1,0:T(8,128)(2,1)S(1)} %all_to_all.15.force_ref, bf16[16,128,256]{2,1,0:T(8,128)(2,1)S(1)} %copy-done.3), custom_call_target="tpu_custom_call" | custom-call | tf_op jit(solution)/shard_map/pallas_call | solution.py:258
  (24 shorter events, 0.4 us)
Async XLA Ops:
  0.0 10.2 %copy-start.1 = (bf16[32,16384]{1,0:T(8,128)(2,1)S(1)}, bf16[32,16384]{1,0:T(8,128)(2,1)}, u32[]{:S(2)}) copy-start(bf16[32,16384]{1,0:T(8,128)(2,1)} %slab_ref.1) | copy-start | bytes 3145732
  1.5 14.4 %all-to-all-start = ((bf16[16,48,128]{2,1,0:T(8,128)(2,1)}), bf16[16,48,128]{2,1,0:T(8,128)(2,1)S(1)}, u32[]{:S(2)}, u32[]{:S(2)}) async-start(bf16[16,48,128]{2,1,0:T(8,128)(2,1)} %shard_map.73), calls=%async_computation | async-start | bytes 393216 | tf_op jit(solution)/shard_map/all_to_all | solution.py:169
  17.7 1.3 %copy-start = (bf16[16,16,32,128]{3,2,1,0:T(8,128)(2,1)}, bf16[16,16,32,128]{3,2,1,0:T(8,128)(2,1)S(1)}, u32[]{:S(2)}) copy-start(bf16[16,16,32,128]{3,2,1,0:T(8,128)(2,1)S(1)} %shard_map.75) | copy-start | bytes 6291460
  19.1 9.0 %copy-start.7 = (s32[512]{0:T(512)S(1)}, s32[512]{0:T(512)}, u32[]{:S(2)}) copy-start(s32[512]{0:T(512)} %param.8) | copy-start | bytes 6148
  19.1 9.0 %copy-start.8 = (f32[512]{0:T(512)S(1)}, f32[512]{0:T(512)}, u32[]{:S(2)}) copy-start(f32[512]{0:T(512)} %param.9) | copy-start | bytes 6148
  19.1 33.3 %all-to-all-start.1 = ((bf16[16,16,32,128]{3,2,1,0:T(8,128)(2,1)}), bf16[16,16,32,128]{3,2,1,0:T(8,128)(2,1)}, u32[]{:S(2)}, u32[]{:S(2)}) async-start(bf16[16,16,32,128]{3,2,1,0:T(8,128)(2,1)} %copy-done), calls=%async_computation.1 | async-start | bytes 4194304 | tf_op jit(solution)/shard_map/all_to_all | solution.py:169
  24.0 2.3 %collective-permute-start = (bf16[16,32,128]{2,1,0:T(8,128)(2,1)S(1)}, bf16[16,32,128]{2,1,0:T(8,128)(2,1)S(1)}, u32[]{:S(2)}, u32[]{:S(2)}) collective-permute-start(bf16[16,32,128]{2,1,0:T(8,128)(2,1)S(1)} %slice_select_fusion), channel_id=1, source_target_pairs={{0,16},{1,17},{2,18},{3,19},{4,20},{5,21},{6,22},{7,23},{8,24},{9,... | collective-permute-start | bytes 393224 | tf_op jit(solution)/shard_map/ppermute | solution.py:202
  26.3 4.8 %collective-permute-start.1 = (bf16[16,32,128]{2,1,0:T(8,128)(2,1)S(1)}, bf16[16,32,128]{2,1,0:T(8,128)(2,1)S(1)}, u32[]{:S(2)}, u32[]{:S(2)}) collective-permute-start(bf16[16,32,128]{2,1,0:T(8,128)(2,1)S(1)} %fusion), channel_id=1, source_target_pairs={{0,32},{16,48},{1,33},{17,49},{2,34},{18,50},{3,35},{19,51},{4,36}... | collective-permute-start | bytes 393224 | tf_op jit(solution)/shard_map/ppermute | solution.py:202
  31.1 3.8 %collective-permute-start.2 = (bf16[16,32,128]{2,1,0:T(8,128)(2,1)S(1)}, bf16[16,32,128]{2,1,0:T(8,128)(2,1)S(1)}, u32[]{:S(2)}, u32[]{:S(2)}) collective-permute-start(bf16[16,32,128]{2,1,0:T(8,128)(2,1)S(1)} %add.16), channel_id=1, source_target_pairs={{0,64},{16,80},{32,96},{48,112},{1,65},{17,81},{33,97},{49,113},{2... | collective-permute-start | bytes 393224 | tf_op jit(solution)/shard_map/ppermute | solution.py:202
  35.1 1.4 %copy-start.4 = (bf16[32,3,64,128]{3,2,1,0:T(8,128)(2,1)S(1)}, bf16[32,3,64,128]{3,2,1,0:T(8,128)(2,1)}, u32[]{:S(2)}) copy-start(bf16[32,3,64,128]{3,2,1,0:T(8,128)(2,1)} %ham_ref) | copy-start | bytes 4718596
  36.5 1.4 %copy-start.5 = (bf16[32,3,64,128]{3,2,1,0:T(8,128)(2,1)S(1)}, bf16[32,3,64,128]{3,2,1,0:T(8,128)(2,1)}, u32[]{:S(2)}) copy-start(bf16[32,3,64,128]{3,2,1,0:T(8,128)(2,1)} %margin_ref) | copy-start | bytes 4718596
  37.9 0.7 copy-start.6
  39.7 1.0 %copy-start.2 = (bf16[16,128,256]{2,1,0:T(8,128)(2,1)}, bf16[16,128,256]{2,1,0:T(8,128)(2,1)S(1)}, u32[]{:S(2)}) copy-start(bf16[16,128,256]{2,1,0:T(8,128)(2,1)S(1)} %shard_map.78.hot_ref) | copy-start | bytes 3145732
  52.4 12.8 %copy-start.3 = (bf16[16,128,256]{2,1,0:T(8,128)(2,1)S(1)}, bf16[16,128,256]{2,1,0:T(8,128)(2,1)}, u32[]{:S(2)}) copy-start(bf16[16,128,256]{2,1,0:T(8,128)(2,1)} %copy-done.2) | copy-start | bytes 3145732

commit v5 on v4

--- a/solution.py
+++ b/solution.py
@@ -6,12 +6,10 @@
 from jax.sharding import PartitionSpec as P
 
 ATOMS_DEV = 160
-ORDER = (0, 1, 2, 3, 4, 5, 6, 7, 8, 9, 10, 11, 12, 13, 14, 15)
-FIRST = (7, 8, 6, 14, 1, 3, 9, 12, 13, 0, 4, 11, 5, 10, 2, 15)
+FIRST = (7, 9, 6, 14, 1, 3, 8, 12, 15, 0, 4, 11, 5, 10, 2, 13)
+BACK = (8, 9, 0, 1, 4, 12, 13, 11, 2, 10, 15, 3, 7, 5, 14, 6)
 HEARD = tuple(FIRST.index(column) for column in range(len(FIRST)))
-BACK = (2, 8, 6, 14, 9, 3, 1, 5, 7, 15, 4, 11, 12, 13, 10, 0)
 RETURN = tuple(BACK.index(column) for column in range(len(BACK)))
-PLACE = tuple(ORDER.index(column) for column in range(len(ORDER)))
 BF16 = jnp.bfloat16
 F32 = jnp.float32
 VMEM = pltpu.VMEM
@@ -42,40 +40,43 @@
     out_ref[:, states:, :] = jnp.broadcast_to(table.astype(F32).astype(BF16)[None], (columns, 16, width))
 
 
-def double_kernel(slab_ref, out_ref):
-    columns, blocks, states, width = out_ref.shape
-    blocks -= 1
+def pack_kernel(table_ref, slab_ref, out_any, doubled_ref, out_ref, sems):
+    columns, homes, states, width = out_ref.shape
     low = lax.broadcasted_iota(jnp.int32, (states, width), 1) < width // 2
-    for place in range(columns):
+    blocks = doubled_ref.shape[1] - 1
+    for place in range(homes):
         for j in range(blocks // 2):
             start = (FIRST[place] * (blocks // 2) + j) * width
             tile = slab_ref[:, start : start + width].astype(F32)
             turned = pltpu.roll(tile, width // 2, 1)
-            out_ref[place, 2 * j] = jnp.where(low, tile, turned).astype(BF16)
-            out_ref[place, 2 * j + 1] = jnp.where(low, turned, tile).astype(BF16)
-        out_ref[place, blocks] = jnp.zeros((states, width), BF16)
-
-
-def pack_kernel(table_ref, doubled_ref, out_ref):
-    columns, homes, states, width = out_ref.shape
-    low = lax.broadcasted_iota(jnp.int32, (states, width), 1) < width // 2
-
-    def home(h, carry):
-        for o in range(columns):
+            doubled_ref[place, 2 * j] = jnp.where(low, tile, turned).astype(BF16)
+            doubled_ref[place, 2 * j + 1] = jnp.where(low, turned, tile).astype(BF16)
+        doubled_ref[place, blocks] = jnp.zeros((states, width), BF16)
+
+    def copy(o):
+        return pltpu.make_async_copy(out_ref.at[o], out_any.at[o], sems.at[o])
+
+    def column(o, carry):
+        for h in range(homes):
             left = doubled_ref[h, table_ref[h, 2 * o]]
             right = doubled_ref[h, table_ref[h, 2 * o + 1]]
-            out_ref[PLACE[o], h] = jnp.where(low, left, right)
+            out_ref[o, h] = jnp.where(low, left, right)
+        copy(o).start()
         return carry
 
-    lax.fori_loop(0, homes, home, 0)
+    def wait(o, carry):
+        copy(o).wait()
+        return carry
+
+    lax.fori_loop(0, columns, column, 0)
+    lax.fori_loop(0, columns, wait, 0)
 
 
 def weights_kernel(panel_ref, scale_ref, out_ref):
     columns, states, width = panel_ref.shape
-    panel = jnp.concatenate([panel_ref[HEARD[column]] for column in ORDER], axis=0).astype(F32).T
-    scale = jnp.concatenate([scale_ref[:, column * states : (column + 1) * states] for column in ORDER], axis=1)
-    out_ref[:width, :] = (panel * scale[0:1, :]).astype(BF16)
-    out_ref[width:, :] = (panel * scale[1:2, :]).astype(BF16)
+    panel = jnp.concatenate([panel_ref[HEARD[column]] for column in range(columns)], axis=0).astype(F32).T
+    out_ref[:width, :] = (panel * scale_ref[0:1, :]).astype(BF16)
+    out_ref[width:, :] = (panel * scale_ref[1:2, :]).astype(BF16)
 
 
 def change_kernel(ham_ref, margin_ref, out_ref):
@@ -176,24 +177,22 @@
         out_shape=jax.ShapeDtypeStruct((columns, states + 16, width), BF16),
     )(tile_owner, eigvec_slab)
     heard = swap(announced, [list(FIRST)])
-    doubled = pl.pallas_call(
-        double_kernel,
-        in_specs=[whole()],
-        out_specs=whole(),
-        out_shape=jax.ShapeDtypeStruct((columns, blocks + 1, states, width), BF16),
-        cost_estimate=pl.CostEstimate(flops=4 << 20, bytes_accessed=3 << 20, transcendentals=0),
-        compiler_params=pltpu.CompilerParams(vmem_limit_bytes=16 << 20),
-    )(eigvec_slab)
-
+    heard, slab = lax.optimization_barrier((heard, eigvec_slab))
     table = heard[:, states, : 2 * columns].astype(jnp.int32)
+    packed_shape = (columns, columns, states, width)
     packed = pl.pallas_call(
         pack_kernel,
         in_specs=[whole(SMEM), whole()],
-        out_specs=whole(),
-        out_shape=jax.ShapeDtypeStruct((columns, columns, states, width), BF16),
+        out_specs=whole(pl.ANY),
+        out_shape=jax.ShapeDtypeStruct(packed_shape, BF16),
+        scratch_shapes=[
+            pltpu.VMEM((columns, blocks + 1, states, width), BF16),
+            pltpu.VMEM(packed_shape, BF16),
+            pltpu.SemaphoreType.DMA((columns,)),
+        ],
         compiler_params=pltpu.CompilerParams(vmem_limit_bytes=16 << 20),
-    )(table, doubled)
-    slabs = swap(packed, [list(ORDER)])
+    )(table, slab)
+    slabs = swap(packed)
 
     panel = heard[:, :states, :]
     panel = jnp.where(row_index == 0, panel, jnp.zeros_like(panel))

time: 66.5 us -> 65.8 us (0.989)
  blocking collectives: 9.83 us -> 23.9 us
  starting transfers between devices: 18 us -> 8.87 us
  waiting for transfers between devices: 22.4 us -> 17.5 us
  local copies, waits for them, and re-layouts: 5.28 us -> 3.97 us
    all_to_all x1 -> x2, blocking collectives: 9.83 us -> 23.9 us  [swap(): lax.all_to_all(x, 'col', split_axis=0, concat_axis=0, tiled=True, axis_in...]
    all_to_all x2 -> x1, starting transfers between devices: 13.6 us -> 4.45 us  [swap(): lax.all_to_all(x, 'col', split_axis=0, concat_axis=0, tiled=True, axis_in...]
    all_to_all x2 -> x1, waiting for transfers between devices: 16.8 us -> 11.9 us  [swap(): lax.all_to_all(x, 'col', split_axis=0, concat_axis=0, tiled=True, axis_in...]
    unnamed x18 -> x16, local copies, waits for them, and re-layouts: 5.21 us -> 3.9 us
    pallas_call x1, Pallas kernels: 1.86 us -> 2.86 us  [per_device(): pl.pallas_call(pack_kernel, in_specs=[whole(SMEM), whole()], out_specs=wh...]
  transfers between devices with their start and end apart: 5 -> 4, of which waited for: 5 -> 4; matrix products, arithmetic and copies ran while one was open for 1% -> 1% of each run, Pallas kernels for 3% -> 3%
where the time goes in v5:
time: 65.8 us; the launch traced here: 65.3 us
  blocking collectives  23.9 us (36%)
  waiting for transfers between devices  17.5 us (27%)
  Pallas kernels  9.95 us (15%)
  starting transfers between devices  8.87 us (13%)
  local copies, waits for them, and re-layouts  3.97 us (6%)
  other arithmetic  0.91 us (1%)
    all_to_all x2, blocking collectives, swap(): lax.all_to_all(x, 'col', split_axis=0, concat_axis=0, tiled=True, axis_in...  23.9 us
    all_to_all x1, waiting for transfers between devices, swap(): lax.all_to_all(x, 'col', split_axis=0, concat_axis=0, tiled=True, axis_in...  11.9 us
    ppermute x3, waiting for transfers between devices, per_device(): lax.ppermute(panel, 'row', [(i, i + reach) for i in range(reach)])  5.55 us
    all_to_all x1, starting transfers between devices, swap(): lax.all_to_all(x, 'col', split_axis=0, concat_axis=0, tiled=True, axis_in...  4.45 us
    ppermute x3, starting transfers between devices, per_device(): lax.ppermute(panel, 'row', [(i, i + reach) for i in range(reach)])  4.42 us
    unnamed x16, local copies, waits for them, and re-layouts  3.9 us
    pallas_call x1, Pallas kernels, per_device(): pl.pallas_call(owner_kernel, in_specs=[whole(pl.ANY), whole(), whole()],...  2.95 us
    pallas_call x1, Pallas kernels, per_device(): pl.pallas_call(pack_kernel, in_specs=[whole(SMEM), whole()], out_specs=wh...  2.86 us
  transfers between devices with their start and end apart: 4, of which 4 were waited for; matrix products, arithmetic and copies ran while one was open for 1% of the time, Pallas kernels for 3%

profile of v5, /device:TPU:0, one launch (start us, length us, event | category | flops | bytes accessed | tf_op | source)
XLA Modules:
  0.0 65.3 jit_solution(14097998797618025369)
XLA Ops:
  0.0 1.5 %shard_map.73 = bf16[16,48,128]{2,1,0:T(8,128)(2,1)} custom-call(s32[16]{0:T(128)} %owner_ref.2, bf16[32,16384]{1,0:T(8,128)(2,1)} %slab_ref), custom_call_target="tpu_custom_call" | custom-call | tf_op jit(solution)/shard_map/pallas_call | solution.py:172
  1.5 14.3 %all_to_all.15 = bf16[16,48,128]{2,1,0:T(8,128)(2,1)S(1)} all-to-all(bf16[16,48,128]{2,1,0:T(8,128)(2,1)} %shard_map.73), channel_id=1, replica_groups={{7,9,6,14,1,3,8,12,15,0,4,11,5,10,2,13},{23,25,22,30,17,19,24,28,31,16,..., dimensions={0} | all-to-all | bytes 393216 | tf_op jit(solution)/shard_map/all_to_all | solution.py:170
  15.9 2.9 %shard_map.74 = bf16[16,16,32,128]{3,2,1,0:T(8,128)(2,1)} custom-call(s32[16,32]{1,0:T(8,128)S(1)} %bitcast.3, bf16[32,16384]{1,0:T(8,128)(2,1)S(1)} %copy-done), custom_call_target="tpu_custom_call" | custom-call | tf_op jit(solution)/shard_map/pallas_call | solution.py:183
  18.8 4.4 %all-to-all-start.1 = ((bf16[16,16,32,128]{3,2,1,0:T(8,128)(2,1)}), bf16[16,16,32,128]{3,2,1,0:T(8,128)(2,1)}, u32[]{:S(2)}, u32[]{:S(2)}) async-start(bf16[16,16,32,128]{3,2,1,0:T(8,128)(2,1)} %shard_map.74), calls=%async_computation.1 | async-start | bytes 4194304 | tf_op jit(solution)/shard_map/all_to_all | solution.py:170
  23.2 1.3 %collective-permute-start = (bf16[16,32,128]{2,1,0:T(8,128)(2,1)S(1)}, bf16[16,32,128]{2,1,0:T(8,128)(2,1)S(1)}, u32[]{:S(2)}, u32[]{:S(2)}) collective-permute-start(bf16[16,32,128]{2,1,0:T(8,128)(2,1)S(1)} %slice_select_fusion), channel_id=1, source_target_pairs={{0,16},{1,17},{2,18},{3,19},{4,20},{5,21},{6,22},{7,23},{8,24},{9,... | collective-permute-start | bytes 393224 | tf_op jit(solution)/shard_map/ppermute | solution.py:201
  24.6 1.0 %collective-permute-done = bf16[16,32,128]{2,1,0:T(8,128)(2,1)S(1)} collective-permute-done((bf16[16,32,128]{2,1,0:T(8,128)(2,1)S(1)}, bf16[16,32,128]{2,1,0:T(8,128)(2,1)S(1)}, u32[]{:S(2)}, u32[]{:S(2)}) %collective-permute-start) | collective-permute-done | bytes 131104 | tf_op jit(solution)/shard_map/ppermute | solution.py:201
  25.5 1.8 %collective-permute-start.1 = (bf16[16,32,128]{2,1,0:T(8,128)(2,1)S(1)}, bf16[16,32,128]{2,1,0:T(8,128)(2,1)S(1)}, u32[]{:S(2)}, u32[]{:S(2)}) collective-permute-start(bf16[16,32,128]{2,1,0:T(8,128)(2,1)S(1)} %fusion), channel_id=1, source_target_pairs={{0,32},{16,48},{1,33},{17,49},{2,34},{18,50},{3,35},{19,51},{4,36}... | collective-permute-start | bytes 393224 | tf_op jit(solution)/shard_map/ppermute | solution.py:201
  27.4 2.9 %collective-permute-done.1 = bf16[16,32,128]{2,1,0:T(8,128)(2,1)S(1)} collective-permute-done((bf16[16,32,128]{2,1,0:T(8,128)(2,1)S(1)}, bf16[16,32,128]{2,1,0:T(8,128)(2,1)S(1)}, u32[]{:S(2)}, u32[]{:S(2)}) %collective-permute-start.1) | collective-permute-done | bytes 131104 | tf_op jit(solution)/shard_map/ppermute | solution.py:201
  30.4 1.3 %collective-permute-start.2 = (bf16[16,32,128]{2,1,0:T(8,128)(2,1)S(1)}, bf16[16,32,128]{2,1,0:T(8,128)(2,1)S(1)}, u32[]{:S(2)}, u32[]{:S(2)}) collective-permute-start(bf16[16,32,128]{2,1,0:T(8,128)(2,1)S(1)} %add.16), channel_id=1, source_target_pairs={{0,64},{16,80},{32,96},{48,112},{1,65},{17,81},{33,97},{49,113},{2... | collective-permute-start | bytes 393224 | tf_op jit(solution)/shard_map/ppermute | solution.py:201
  31.7 0.7 %dynamic-slice_subtract_fusion = s32[1024]{0:T(1024)S(1)} fusion(s32[131072]{0:T(1024)} %param.13, s32[]{:T(128)S(6)} %select_n.13, s32[]{:T(128)S(6)} %mul.16), kind=kLoop, calls=%fused_computation.4 | loop fusion | flops 1024 | bytes 8200 | tf_op jit(solution)/shard_map/sub | solution.py:220
  32.4 0.1 reshape.5
  32.5 0.1 pad_add_fusion.atom_ref
  32.6 1.6 %collective-permute-done.2 = bf16[16,32,128]{2,1,0:T(8,128)(2,1)S(1)} collective-permute-done((bf16[16,32,128]{2,1,0:T(8,128)(2,1)S(1)}, bf16[16,32,128]{2,1,0:T(8,128)(2,1)S(1)}, u32[]{:S(2)}, u32[]{:S(2)}) %collective-permute-start.2) | collective-permute-done | bytes 131104 | tf_op jit(solution)/shard_map/ppermute | solution.py:201
  34.3 0.1 shard_map.75.weights_ref
  34.4 1.4 %copy-done.3 = bf16[32,3,64,128]{3,2,1,0:T(8,128)(2,1)S(1)} copy-done((bf16[32,3,64,128]{3,2,1,0:T(8,128)(2,1)S(1)}, bf16[32,3,64,128]{3,2,1,0:T(8,128)(2,1)}, u32[]{:S(2)}) %copy-start.3) | copy-done | bytes 1572888
  35.8 1.4 %copy-done.4 = bf16[32,3,64,128]{3,2,1,0:T(8,128)(2,1)S(1)} copy-done((bf16[32,3,64,128]{3,2,1,0:T(8,128)(2,1)S(1)}, bf16[32,3,64,128]{3,2,1,0:T(8,128)(2,1)}, u32[]{:S(2)}) %copy-start.4) | copy-done | bytes 1572888
  37.2 0.5 shard_map.76.change_ref
  37.7 0.1 copy-done.5
  37.8 1.2 %shard_map.77.hot_ref = bf16[16,128,256]{2,1,0:T(8,128)(2,1)S(1)} custom-call(s32[16]{0:T(128)S(1)} %copy-done.5, s32[16,128]{1,0:T(8,128)S(1)} %pad_add_fusion.atom_ref), custom_call_target="tpu_custom_call" | custom-call | flops 4194304 | bytes 1048576 | tf_op jit(solution)/shard_map/pallas_call | solution.py:223
  39.0 1.0 %copy-done.1 = bf16[16,128,256]{2,1,0:T(8,128)(2,1)} copy-done((bf16[16,128,256]{2,1,0:T(8,128)(2,1)}, bf16[16,128,256]{2,1,0:T(8,128)(2,1)S(1)}, u32[]{:S(2)}) %copy-start.1) | copy-done | bytes 1048600
  40.0 11.9 %all-to-all-done.1.slab_any = bf16[16,16,32,128]{3,2,1,0:T(8,128)(2,1)} async-done(((bf16[16,16,32,128]{3,2,1,0:T(8,128)(2,1)}), bf16[16,16,32,128]{3,2,1,0:T(8,128)(2,1)}, u32[]{:S(2)}, u32[]{:S(2)}) %all-to-all-start.1) | async-done | bytes 2097184 | tf_op jit(solution)/shard_map/all_to_all | solution.py:170
  51.9 2.9 %shard_map.78 = bf16[16,16,128]{2,1,0:T(8,128)(2,1)S(1)} custom-call(bf16[16,16,32,128]{3,2,1,0:T(8,128)(2,1)} %all-to-all-done.1.slab_any, bf16[256,512]{1,0:T(8,128)(2,1)S(1)} %shard_map.75.weights_ref, bf16[16,384,256]{2,1,0:T(8,128)(2,1)S(1)} %shard_map.76.change_ref), custom_call_target="tpu_custom_call" | custom-call | tf_op jit(solution)/shard_map/pallas_call | solution.py:242
  54.8 9.6 %all_to_all.16.force_ref = bf16[16,16,128]{2,1,0:T(8,128)(2,1)S(1)} all-to-all(bf16[16,16,128]{2,1,0:T(8,128)(2,1)S(1)} %shard_map.78), channel_id=1, replica_groups={{8,9,0,1,4,12,13,11,2,10,15,3,7,5,14,6},{24,25,16,17,20,28,29,27,18,26,..., dimensions={0} | all-to-all | bytes 131072 | tf_op jit(solution)/shard_map/all_to_all | solution.py:170
  64.4 0.8 %shard_map.79 = f32[3,160]{1,0:T(4,128)} custom-call(bf16[16,16,128]{2,1,0:T(8,128)(2,1)S(1)} %all_to_all.16.force_ref, bf16[16,128,256]{2,1,0:T(8,128)(2,1)S(1)} %copy-done.2), custom_call_target="tpu_custom_call" | custom-call | tf_op jit(solution)/shard_map/pallas_call | solution.py:257
  (20 shorter events, 0.2 us)
Async XLA Ops:
  0.0 15.9 %copy-start = (bf16[32,16384]{1,0:T(8,128)(2,1)S(1)}, bf16[32,16384]{1,0:T(8,128)(2,1)}, u32[]{:S(2)}) copy-start(bf16[32,16384]{1,0:T(8,128)(2,1)} %slab_ref) | copy-start | bytes 3145732
  18.7 8.6 %copy-start.6 = (s32[512]{0:T(512)S(1)}, s32[512]{0:T(512)}, u32[]{:S(2)}) copy-start(s32[512]{0:T(512)} %param.8) | copy-start | bytes 6148
  18.7 8.6 %copy-start.7 = (f32[512]{0:T(512)S(1)}, f32[512]{0:T(512)}, u32[]{:S(2)}) copy-start(f32[512]{0:T(512)} %param.9) | copy-start | bytes 6148
  18.8 33.1 %all-to-all-start.1 = ((bf16[16,16,32,128]{3,2,1,0:T(8,128)(2,1)}), bf16[16,16,32,128]{3,2,1,0:T(8,128)(2,1)}, u32[]{:S(2)}, u32[]{:S(2)}) async-start(bf16[16,16,32,128]{3,2,1,0:T(8,128)(2,1)} %shard_map.74), calls=%async_computation.1 | async-start | bytes 4194304 | tf_op jit(solution)/shard_map/all_to_all | solution.py:170
  23.2 2.3 %collective-permute-start = (bf16[16,32,128]{2,1,0:T(8,128)(2,1)S(1)}, bf16[16,32,128]{2,1,0:T(8,128)(2,1)S(1)}, u32[]{:S(2)}, u32[]{:S(2)}) collective-permute-start(bf16[16,32,128]{2,1,0:T(8,128)(2,1)S(1)} %slice_select_fusion), channel_id=1, source_target_pairs={{0,16},{1,17},{2,18},{3,19},{4,20},{5,21},{6,22},{7,23},{8,24},{9,... | collective-permute-start | bytes 393224 | tf_op jit(solution)/shard_map/ppermute | solution.py:201
  25.5 4.8 %collective-permute-start.1 = (bf16[16,32,128]{2,1,0:T(8,128)(2,1)S(1)}, bf16[16,32,128]{2,1,0:T(8,128)(2,1)S(1)}, u32[]{:S(2)}, u32[]{:S(2)}) collective-permute-start(bf16[16,32,128]{2,1,0:T(8,128)(2,1)S(1)} %fusion), channel_id=1, source_target_pairs={{0,32},{16,48},{1,33},{17,49},{2,34},{18,50},{3,35},{19,51},{4,36}... | collective-permute-start | bytes 393224 | tf_op jit(solution)/shard_map/ppermute | solution.py:201
  30.4 3.8 %collective-permute-start.2 = (bf16[16,32,128]{2,1,0:T(8,128)(2,1)S(1)}, bf16[16,32,128]{2,1,0:T(8,128)(2,1)S(1)}, u32[]{:S(2)}, u32[]{:S(2)}) collective-permute-start(bf16[16,32,128]{2,1,0:T(8,128)(2,1)S(1)} %add.16), channel_id=1, source_target_pairs={{0,64},{16,80},{32,96},{48,112},{1,65},{17,81},{33,97},{49,113},{2... | collective-permute-start | bytes 393224 | tf_op jit(solution)/shard_map/ppermute | solution.py:201
  34.4 1.4 %copy-start.3 = (bf16[32,3,64,128]{3,2,1,0:T(8,128)(2,1)S(1)}, bf16[32,3,64,128]{3,2,1,0:T(8,128)(2,1)}, u32[]{:S(2)}) copy-start(bf16[32,3,64,128]{3,2,1,0:T(8,128)(2,1)} %ham_ref) | copy-start | bytes 4718596
  35.8 1.4 %copy-start.4 = (bf16[32,3,64,128]{3,2,1,0:T(8,128)(2,1)S(1)}, bf16[32,3,64,128]{3,2,1,0:T(8,128)(2,1)}, u32[]{:S(2)}) copy-start(bf16[32,3,64,128]{3,2,1,0:T(8,128)(2,1)} %margin_ref) | copy-start | bytes 4718596
  37.2 0.7 %copy-start.5 = (s32[16]{0:T(128)S(1)}, s32[16]{0:T(128)}, u32[]{:S(2)}) copy-start(s32[16]{0:T(128)} %owner_ref.2) | copy-start | bytes 196
  39.0 1.0 %copy-start.1 = (bf16[16,128,256]{2,1,0:T(8,128)(2,1)}, bf16[16,128,256]{2,1,0:T(8,128)(2,1)S(1)}, u32[]{:S(2)}) copy-start(bf16[16,128,256]{2,1,0:T(8,128)(2,1)S(1)} %shard_map.77.hot_ref) | copy-start | bytes 3145732
  51.9 12.6 %copy-start.2 = (bf16[16,128,256]{2,1,0:T(8,128)(2,1)S(1)}, bf16[16,128,256]{2,1,0:T(8,128)(2,1)}, u32[]{:S(2)}) copy-start(bf16[16,128,256]{2,1,0:T(8,128)(2,1)} %copy-done.1) | copy-start | bytes 3145732

commit v6 on v5

--- a/solution.py
+++ b/solution.py
@@ -40,10 +40,12 @@
     out_ref[:, states:, :] = jnp.broadcast_to(table.astype(F32).astype(BF16)[None], (columns, 16, width))
 
 
-def pack_kernel(table_ref, slab_ref, out_any, doubled_ref, out_ref, sems):
+def pack_kernel(table_any, slab_ref, out_any, table_ref, doubled_ref, out_ref, sems):
     columns, homes, states, width = out_ref.shape
     low = lax.broadcasted_iota(jnp.int32, (states, width), 1) < width // 2
     blocks = doubled_ref.shape[1] - 1
+    table = pltpu.make_async_copy(table_any, table_ref, sems.at[columns])
+    table.start()
     for place in range(homes):
         for j in range(blocks // 2):
             start = (FIRST[place] * (blocks // 2) + j) * width
@@ -68,6 +70,7 @@
         copy(o).wait()
         return carry
 
+    table.wait()
     lax.fori_loop(0, columns, column, 0)
     lax.fori_loop(0, columns, wait, 0)
 
@@ -182,13 +185,14 @@
     packed_shape = (columns, columns, states, width)
     packed = pl.pallas_call(
         pack_kernel,
-        in_specs=[whole(SMEM), whole()],
+        in_specs=[whole(pl.ANY), whole()],
         out_specs=whole(pl.ANY),
         out_shape=jax.ShapeDtypeStruct(packed_shape, BF16),
         scratch_shapes=[
+            pltpu.SMEM(table.shape, jnp.int32),
             pltpu.VMEM((columns, blocks + 1, states, width), BF16),
             pltpu.VMEM(packed_shape, BF16),
-            pltpu.SemaphoreType.DMA((columns,)),
+            pltpu.SemaphoreType.DMA((columns + 1,)),
         ],
         compiler_params=pltpu.CompilerParams(vmem_limit_bytes=16 << 20),
     )(table, slab)

time: 65.8 us -> 65.3 us (level)
  transfers between devices with their start and end apart: 4 -> 4, of which waited for: 4 -> 4; matrix products, arithmetic and copies ran while one was open for 1% -> 2% of each run, Pallas kernels for 3% -> 3%
where the time goes in v6:
time: 65.3 us; the launch traced here: 64.9 us
  blocking collectives  23.9 us (37%)
  waiting for transfers between devices  17.5 us (27%)
  Pallas kernels  9.54 us (15%)
  starting transfers between devices  8.87 us (14%)
  local copies, waits for them, and re-layouts  3.97 us (6%)
  other arithmetic  0.91 us (1%)
    all_to_all x2, blocking collectives, swap(): lax.all_to_all(x, 'col', split_axis=0, concat_axis=0, tiled=True, axis_in...  23.9 us
    all_to_all x1, waiting for transfers between devices, swap(): lax.all_to_all(x, 'col', split_axis=0, concat_axis=0, tiled=True, axis_in...  11.9 us
    ppermute x3, waiting for transfers between devices, per_device(): lax.ppermute(panel, 'row', [(i, i + reach) for i in range(reach)])  5.55 us
    all_to_all x1, starting transfers between devices, swap(): lax.all_to_all(x, 'col', split_axis=0, concat_axis=0, tiled=True, axis_in...  4.45 us
    ppermute x3, starting transfers between devices, per_device(): lax.ppermute(panel, 'row', [(i, i + reach) for i in range(reach)])  4.42 us
    unnamed x16, local copies, waits for them, and re-layouts  3.9 us
    pallas_call x1, Pallas kernels, per_device(): pl.pallas_call(owner_kernel, in_specs=[whole(pl.ANY), whole(), whole()],...  2.95 us
    pallas_call x1, Pallas kernels, per_device(): pl.pallas_call(pack_kernel, in_specs=[whole(pl.ANY), whole()], out_specs=...  2.44 us
  transfers between devices with their start and end apart: 4, of which 4 were waited for; matrix products, arithmetic and copies ran while one was open for 2% of the time, Pallas kernels for 3%

profile of v6, /device:TPU:0, one launch (start us, length us, event | category | flops | bytes accessed | tf_op | source)
XLA Modules:
  0.0 64.9 jit_solution(10288573098734385557)
XLA Ops:
  0.0 1.5 %shard_map.73 = bf16[16,48,128]{2,1,0:T(8,128)(2,1)} custom-call(s32[16]{0:T(128)} %owner_ref.2, bf16[32,16384]{1,0:T(8,128)(2,1)} %slab_ref), custom_call_target="tpu_custom_call" | custom-call | tf_op jit(solution)/shard_map/pallas_call | solution.py:175
  1.5 14.3 %all_to_all.15 = bf16[16,48,128]{2,1,0:T(8,128)(2,1)S(1)} all-to-all(bf16[16,48,128]{2,1,0:T(8,128)(2,1)} %shard_map.73), channel_id=1, replica_groups={{7,9,6,14,1,3,8,12,15,0,4,11,5,10,2,13},{23,25,22,30,17,19,24,28,31,16,..., dimensions={0} | all-to-all | bytes 393216 | tf_op jit(solution)/shard_map/all_to_all | solution.py:173
  15.9 2.4 %shard_map.74 = bf16[16,16,32,128]{3,2,1,0:T(8,128)(2,1)} custom-call(s32[16,32]{1,0:T(8,128)S(1)} %bitcast.3, bf16[32,16384]{1,0:T(8,128)(2,1)S(1)} %copy-done), custom_call_target="tpu_custom_call" | custom-call | tf_op jit(solution)/shard_map/pallas_call | solution.py:186
  18.3 4.4 %all-to-all-start.1 = ((bf16[16,16,32,128]{3,2,1,0:T(8,128)(2,1)}), bf16[16,16,32,128]{3,2,1,0:T(8,128)(2,1)}, u32[]{:S(2)}, u32[]{:S(2)}) async-start(bf16[16,16,32,128]{3,2,1,0:T(8,128)(2,1)} %shard_map.74), calls=%async_computation.1 | async-start | bytes 4194304 | tf_op jit(solution)/shard_map/all_to_all | solution.py:173
  22.8 1.3 %collective-permute-start = (bf16[16,32,128]{2,1,0:T(8,128)(2,1)S(1)}, bf16[16,32,128]{2,1,0:T(8,128)(2,1)S(1)}, u32[]{:S(2)}, u32[]{:S(2)}) collective-permute-start(bf16[16,32,128]{2,1,0:T(8,128)(2,1)S(1)} %slice_select_fusion), channel_id=1, source_target_pairs={{0,16},{1,17},{2,18},{3,19},{4,20},{5,21},{6,22},{7,23},{8,24},{9,... | collective-permute-start | bytes 393224 | tf_op jit(solution)/shard_map/ppermute | solution.py:205
  24.1 1.0 %collective-permute-done = bf16[16,32,128]{2,1,0:T(8,128)(2,1)S(1)} collective-permute-done((bf16[16,32,128]{2,1,0:T(8,128)(2,1)S(1)}, bf16[16,32,128]{2,1,0:T(8,128)(2,1)S(1)}, u32[]{:S(2)}, u32[]{:S(2)}) %collective-permute-start) | collective-permute-done | bytes 131104 | tf_op jit(solution)/shard_map/ppermute | solution.py:205
  25.1 1.8 %collective-permute-start.1 = (bf16[16,32,128]{2,1,0:T(8,128)(2,1)S(1)}, bf16[16,32,128]{2,1,0:T(8,128)(2,1)S(1)}, u32[]{:S(2)}, u32[]{:S(2)}) collective-permute-start(bf16[16,32,128]{2,1,0:T(8,128)(2,1)S(1)} %fusion), channel_id=1, source_target_pairs={{0,32},{16,48},{1,33},{17,49},{2,34},{18,50},{3,35},{19,51},{4,36}... | collective-permute-start | bytes 393224 | tf_op jit(solution)/shard_map/ppermute | solution.py:205
  27.0 2.9 %collective-permute-done.1 = bf16[16,32,128]{2,1,0:T(8,128)(2,1)S(1)} collective-permute-done((bf16[16,32,128]{2,1,0:T(8,128)(2,1)S(1)}, bf16[16,32,128]{2,1,0:T(8,128)(2,1)S(1)}, u32[]{:S(2)}, u32[]{:S(2)}) %collective-permute-start.1) | collective-permute-done | bytes 131104 | tf_op jit(solution)/shard_map/ppermute | solution.py:205
  30.0 1.3 %collective-permute-start.2 = (bf16[16,32,128]{2,1,0:T(8,128)(2,1)S(1)}, bf16[16,32,128]{2,1,0:T(8,128)(2,1)S(1)}, u32[]{:S(2)}, u32[]{:S(2)}) collective-permute-start(bf16[16,32,128]{2,1,0:T(8,128)(2,1)S(1)} %add.16), channel_id=1, source_target_pairs={{0,64},{16,80},{32,96},{48,112},{1,65},{17,81},{33,97},{49,113},{2... | collective-permute-start | bytes 393224 | tf_op jit(solution)/shard_map/ppermute | solution.py:205
  31.3 0.7 %dynamic-slice_subtract_fusion = s32[1024]{0:T(1024)S(1)} fusion(s32[131072]{0:T(1024)} %param.13, s32[]{:T(128)S(6)} %select_n.13, s32[]{:T(128)S(6)} %mul.16), kind=kLoop, calls=%fused_computation.4 | loop fusion | flops 1024 | bytes 8200 | tf_op jit(solution)/shard_map/sub | solution.py:224
  32.0 0.1 reshape.5
  32.1 0.1 pad_add_fusion.atom_ref
  32.2 1.6 %collective-permute-done.2 = bf16[16,32,128]{2,1,0:T(8,128)(2,1)S(1)} collective-permute-done((bf16[16,32,128]{2,1,0:T(8,128)(2,1)S(1)}, bf16[16,32,128]{2,1,0:T(8,128)(2,1)S(1)}, u32[]{:S(2)}, u32[]{:S(2)}) %collective-permute-start.2) | collective-permute-done | bytes 131104 | tf_op jit(solution)/shard_map/ppermute | solution.py:205
  33.8 0.1 shard_map.75.weights_ref
  34.0 1.4 %copy-done.3 = bf16[32,3,64,128]{3,2,1,0:T(8,128)(2,1)S(1)} copy-done((bf16[32,3,64,128]{3,2,1,0:T(8,128)(2,1)S(1)}, bf16[32,3,64,128]{3,2,1,0:T(8,128)(2,1)}, u32[]{:S(2)}) %copy-start.3) | copy-done | bytes 1572888
  35.4 1.4 %copy-done.4 = bf16[32,3,64,128]{3,2,1,0:T(8,128)(2,1)S(1)} copy-done((bf16[32,3,64,128]{3,2,1,0:T(8,128)(2,1)S(1)}, bf16[32,3,64,128]{3,2,1,0:T(8,128)(2,1)}, u32[]{:S(2)}) %copy-start.4) | copy-done | bytes 1572888
  36.8 0.5 shard_map.76.change_ref
  37.3 0.1 copy-done.5
  37.4 1.2 %shard_map.77.hot_ref = bf16[16,128,256]{2,1,0:T(8,128)(2,1)S(1)} custom-call(s32[16]{0:T(128)S(1)} %copy-done.5, s32[16,128]{1,0:T(8,128)S(1)} %pad_add_fusion.atom_ref), custom_call_target="tpu_custom_call" | custom-call | flops 4194304 | bytes 1048576 | tf_op jit(solution)/shard_map/pallas_call | solution.py:227
  38.6 1.0 %copy-done.1 = bf16[16,128,256]{2,1,0:T(8,128)(2,1)} copy-done((bf16[16,128,256]{2,1,0:T(8,128)(2,1)}, bf16[16,128,256]{2,1,0:T(8,128)(2,1)S(1)}, u32[]{:S(2)}) %copy-start.1) | copy-done | bytes 1048600
  39.6 11.9 %all-to-all-done.1.slab_any = bf16[16,16,32,128]{3,2,1,0:T(8,128)(2,1)} async-done(((bf16[16,16,32,128]{3,2,1,0:T(8,128)(2,1)}), bf16[16,16,32,128]{3,2,1,0:T(8,128)(2,1)}, u32[]{:S(2)}, u32[]{:S(2)}) %all-to-all-start.1) | async-done | bytes 2097184 | tf_op jit(solution)/shard_map/all_to_all | solution.py:173
  51.5 2.9 %shard_map.78 = bf16[16,16,128]{2,1,0:T(8,128)(2,1)S(1)} custom-call(bf16[16,16,32,128]{3,2,1,0:T(8,128)(2,1)} %all-to-all-done.1.slab_any, bf16[256,512]{1,0:T(8,128)(2,1)S(1)} %shard_map.75.weights_ref, bf16[16,384,256]{2,1,0:T(8,128)(2,1)S(1)} %shard_map.76.change_ref), custom_call_target="tpu_custom_call" | custom-call | tf_op jit(solution)/shard_map/pallas_call | solution.py:246
  54.4 9.6 %all_to_all.16.force_ref = bf16[16,16,128]{2,1,0:T(8,128)(2,1)S(1)} all-to-all(bf16[16,16,128]{2,1,0:T(8,128)(2,1)S(1)} %shard_map.78), channel_id=1, replica_groups={{8,9,0,1,4,12,13,11,2,10,15,3,7,5,14,6},{24,25,16,17,20,28,29,27,18,26,..., dimensions={0} | all-to-all | bytes 131072 | tf_op jit(solution)/shard_map/all_to_all | solution.py:173
  64.0 0.8 %shard_map.79 = f32[3,160]{1,0:T(4,128)} custom-call(bf16[16,16,128]{2,1,0:T(8,128)(2,1)S(1)} %all_to_all.16.force_ref, bf16[16,128,256]{2,1,0:T(8,128)(2,1)S(1)} %copy-done.2), custom_call_target="tpu_custom_call" | custom-call | tf_op jit(solution)/shard_map/pallas_call | solution.py:261
  (20 shorter events, 0.2 us)
Async XLA Ops:
  0.0 15.9 %copy-start = (bf16[32,16384]{1,0:T(8,128)(2,1)S(1)}, bf16[32,16384]{1,0:T(8,128)(2,1)}, u32[]{:S(2)}) copy-start(bf16[32,16384]{1,0:T(8,128)(2,1)} %slab_ref) | copy-start | bytes 3145732
  18.3 8.6 %copy-start.6 = (s32[512]{0:T(512)S(1)}, s32[512]{0:T(512)}, u32[]{:S(2)}) copy-start(s32[512]{0:T(512)} %param.8) | copy-start | bytes 6148
  18.3 8.6 %copy-start.7 = (f32[512]{0:T(512)S(1)}, f32[512]{0:T(512)}, u32[]{:S(2)}) copy-start(f32[512]{0:T(512)} %param.9) | copy-start | bytes 6148
  18.3 33.1 %all-to-all-start.1 = ((bf16[16,16,32,128]{3,2,1,0:T(8,128)(2,1)}), bf16[16,16,32,128]{3,2,1,0:T(8,128)(2,1)}, u32[]{:S(2)}, u32[]{:S(2)}) async-start(bf16[16,16,32,128]{3,2,1,0:T(8,128)(2,1)} %shard_map.74), calls=%async_computation.1 | async-start | bytes 4194304 | tf_op jit(solution)/shard_map/all_to_all | solution.py:173
  22.8 2.3 %collective-permute-start = (bf16[16,32,128]{2,1,0:T(8,128)(2,1)S(1)}, bf16[16,32,128]{2,1,0:T(8,128)(2,1)S(1)}, u32[]{:S(2)}, u32[]{:S(2)}) collective-permute-start(bf16[16,32,128]{2,1,0:T(8,128)(2,1)S(1)} %slice_select_fusion), channel_id=1, source_target_pairs={{0,16},{1,17},{2,18},{3,19},{4,20},{5,21},{6,22},{7,23},{8,24},{9,... | collective-permute-start | bytes 393224 | tf_op jit(solution)/shard_map/ppermute | solution.py:205
  25.1 4.8 %collective-permute-start.1 = (bf16[16,32,128]{2,1,0:T(8,128)(2,1)S(1)}, bf16[16,32,128]{2,1,0:T(8,128)(2,1)S(1)}, u32[]{:S(2)}, u32[]{:S(2)}) collective-permute-start(bf16[16,32,128]{2,1,0:T(8,128)(2,1)S(1)} %fusion), channel_id=1, source_target_pairs={{0,32},{16,48},{1,33},{17,49},{2,34},{18,50},{3,35},{19,51},{4,36}... | collective-permute-start | bytes 393224 | tf_op jit(solution)/shard_map/ppermute | solution.py:205
  30.0 3.8 %collective-permute-start.2 = (bf16[16,32,128]{2,1,0:T(8,128)(2,1)S(1)}, bf16[16,32,128]{2,1,0:T(8,128)(2,1)S(1)}, u32[]{:S(2)}, u32[]{:S(2)}) collective-permute-start(bf16[16,32,128]{2,1,0:T(8,128)(2,1)S(1)} %add.16), channel_id=1, source_target_pairs={{0,64},{16,80},{32,96},{48,112},{1,65},{17,81},{33,97},{49,113},{2... | collective-permute-start | bytes 393224 | tf_op jit(solution)/shard_map/ppermute | solution.py:205
  34.0 1.4 %copy-start.3 = (bf16[32,3,64,128]{3,2,1,0:T(8,128)(2,1)S(1)}, bf16[32,3,64,128]{3,2,1,0:T(8,128)(2,1)}, u32[]{:S(2)}) copy-start(bf16[32,3,64,128]{3,2,1,0:T(8,128)(2,1)} %ham_ref) | copy-start | bytes 4718596
  35.4 1.4 %copy-start.4 = (bf16[32,3,64,128]{3,2,1,0:T(8,128)(2,1)S(1)}, bf16[32,3,64,128]{3,2,1,0:T(8,128)(2,1)}, u32[]{:S(2)}) copy-start(bf16[32,3,64,128]{3,2,1,0:T(8,128)(2,1)} %margin_ref) | copy-start | bytes 4718596
  36.8 0.7 %copy-start.5 = (s32[16]{0:T(128)S(1)}, s32[16]{0:T(128)}, u32[]{:S(2)}) copy-start(s32[16]{0:T(128)} %owner_ref.2) | copy-start | bytes 196
  38.6 1.0 %copy-start.1 = (bf16[16,128,256]{2,1,0:T(8,128)(2,1)}, bf16[16,128,256]{2,1,0:T(8,128)(2,1)S(1)}, u32[]{:S(2)}) copy-start(bf16[16,128,256]{2,1,0:T(8,128)(2,1)S(1)} %shard_map.77.hot_ref) | copy-start | bytes 3145732
  51.5 12.6 %copy-start.2 = (bf16[16,128,256]{2,1,0:T(8,128)(2,1)S(1)}, bf16[16,128,256]{2,1,0:T(8,128)(2,1)}, u32[]{:S(2)}) copy-start(bf16[16,128,256]{2,1,0:T(8,128)(2,1)} %copy-done.1) | copy-start | bytes 3145732
